TPU v7x, 256 devices: a whole 4x4x8 slice. The times are simulated.
256 devices in a mesh: frame: 32 (over x, z_lo, core), tok: 8 (over y, z_hi).
Axes of the slice: x: 4, y: 4, z: 8 (z_hi: 2, z_lo: 4; z = z_hi * 4 + z_lo), core: 2. Of those that a mesh axis runs over, the one named last changes fastest.
Arguments:
- patches: bfloat16 [32, 1024, 1408], P('frame', 'tok'), may hold values from -6 to 6
- shift_offset: int32 [1024], P('tok'), may hold values from -1 to 1
- shift_slice: int32 [1024], P('tok'), may hold values from 0 to 3
- w_query: bfloat16 [1408, 1408], P('frame', 'tok'), may hold values from -0.15625 to 0.15625
- w_key: bfloat16 [1408, 1408], P('frame', 'tok'), may hold values from -0.15625 to 0.15625
- w_value: bfloat16 [1408, 1408], P('frame', 'tok'), may hold values from -0.15625 to 0.15625
- w_out: bfloat16 [1408, 1408], P('tok', 'frame'), may hold values from -1.25 to 1.25
- w_up: bfloat16 [1408, 6144], P('frame', 'tok'), may hold values from -0.15625 to 0.15625
- w_down: bfloat16 [6144, 1408], P('tok', 'frame'), may hold values from -0.078125 to 0.078125
- t_query: bfloat16 [1408, 1408], P('tok'), may hold values from -0.15625 to 0.15625
- t_key: bfloat16 [1408, 1408], P('tok'), may hold values from -0.15625 to 0.15625
- t_value: bfloat16 [1408, 1408], P('tok'), may hold values from -0.15625 to 0.15625
- t_out: bfloat16 [1408, 1408], P('tok'), may hold values from -0.15625 to 0.15625
- cache_keys: bfloat16 [1984, 1408], P('frame', 'tok'), may hold values from -6 to 6
- cache_values: bfloat16 [1984, 1408], P('frame', 'tok'), may hold values from -6 to 6
- cache_pos: int32 [1984], P('frame'), may hold values from 0 to 4095
Outputs:
- patch_out: bfloat16 [32, 1024, 1408], P('frame', 'tok')
- frame_out: bfloat16 [32, 1408], P('frame', 'tok')
Inputs may be any that keep to these rules, and one draw needn't show every extreme that they name: `shift_offset`: -1 takes channels from the frame before, 1 from the frame after, 0 none. `cache_pos`: all cached positions lie before the new frames.
All inputs are finite; a program needn't handle non-finite values.
Results may differ from a plain program's by a relative error of at most 0.018.
Values may be sent and summed in bfloat16 or wider, within the bound.
A program may use at most 64 MiB of HBM per device.

v0:
```python
import jax
import jax.numpy as jnp
from jax import lax
from jax.sharding import PartitionSpec as P

HEADS = 16
HD = 88
P_SIZE = 1024
SPAN = 4096


def from_behind(block, axis, distance):
    devices = range(lax.axis_size(axis))
    route = [(i - distance, i) for i in devices if i - distance in devices]
    return lax.ppermute(block, axis, route)


def layer_norm(values):
    center = values - jnp.mean(values, axis=-1, keepdims=True)
    spread = jnp.mean(center * center, axis=-1, keepdims=True)
    return center * lax.rsqrt(spread + 1e-06)


def rotate(values, positions):
    half = values.shape[-1] // 2
    freq = 10000.0 ** (-jnp.arange(half, dtype=jnp.float32) / half)
    angle = positions[:, None, None] * freq[None, None, :]
    first = values[..., :half]
    second = values[..., half:]
    cosine = jnp.cos(angle)
    sine = jnp.sin(angle)
    return jnp.concatenate(
        [first * cosine - second * sine, first * sine + second * cosine], axis=-1
    )


def add_rows(left, piece):
    return jnp.dot(left, piece, preferred_element_type=jnp.float32)


def spatial(query, key, value):
    scale = HD ** (-0.5)
    heads = query.shape[1] // HD
    results = []
    for head in range(heads):
        lower = head * HD
        q_part = query[:, lower : lower + HD]
        k_part = key[:, lower : lower + HD]
        v_part = value[:, lower : lower + HD]
        scores = jnp.dot(q_part, k_part.T, preferred_element_type=jnp.float32) * scale
        weights = jax.nn.softmax(scores, axis=-1).astype(jnp.bfloat16)
        results.append(
            jnp.dot(weights, v_part, preferred_element_type=jnp.float32).astype(jnp.bfloat16)
        )
    return jnp.concatenate(results, axis=1)


def body(
    patches,
    shift_offset,
    shift_slice,
    w_query,
    w_key,
    w_value,
    w_out,
    w_up,
    w_down,
    t_query,
    t_key,
    t_value,
    t_out,
    cache_keys,
    cache_values,
    cache_pos,
):
    residual = patches[0].astype(jnp.float32)
    width = residual.shape[1]
    normed = layer_norm(residual).astype(jnp.bfloat16)
    earlier = from_behind(normed, "frame", 1)
    later = from_behind(normed, "frame", -1)
    offsets = shift_offset[:, None]
    source = jnp.where(offsets == -1, earlier, jnp.where(offsets == 1, later, normed))
    quarter = jnp.arange(width, dtype=jnp.int32) // (width // 4)
    chosen = quarter[None, :] == shift_slice[:, None]
    shifted = jnp.where(chosen, source, normed)
    frame_rows = lax.all_gather(shifted, "tok", axis=0, tiled=True)

    def add_one(piece):
        return add_rows(frame_rows, piece)

    query = add_one(lax.all_gather(w_query, "frame", axis=0, tiled=True))
    key = add_one(lax.all_gather(w_key, "frame", axis=0, tiled=True))
    value = add_one(lax.all_gather(w_value, "frame", axis=0, tiled=True))
    attended = spatial(
        query.astype(jnp.bfloat16), key.astype(jnp.bfloat16), value.astype(jnp.bfloat16)
    )
    projected = jnp.dot(
        attended,
        lax.all_gather(w_out, "frame", axis=1, tiled=True),
        preferred_element_type=jnp.float32,
    )
    attention_sum = lax.psum_scatter(
        projected.astype(jnp.bfloat16), "tok", scatter_dimension=0, tiled=True
    ).astype(jnp.float32)
    mixed = (residual + attention_sum).astype(jnp.bfloat16)
    second = layer_norm(mixed.astype(jnp.float32)).astype(jnp.bfloat16)
    second_rows = lax.all_gather(second, "tok", axis=0, tiled=True)
    up_sum = add_rows(second_rows, lax.all_gather(w_up, "frame", axis=0, tiled=True))
    hidden = jax.nn.gelu(up_sum).astype(jnp.bfloat16)
    down_terms = jnp.dot(
        hidden,
        lax.all_gather(w_down, "frame", axis=1, tiled=True),
        preferred_element_type=jnp.float32,
    )
    mlp_sum = lax.psum_scatter(
        down_terms.astype(jnp.bfloat16), "tok", scatter_dimension=0, tiled=True
    ).astype(jnp.float32)
    result = (mixed.astype(jnp.float32) + mlp_sum).astype(jnp.bfloat16)
    frame_index = lax.axis_index("frame")
    tok_index = lax.axis_index("tok")
    pooled = lax.psum(jnp.sum(result.astype(jnp.float32), axis=0), "tok") / P_SIZE
    pooled_normed = layer_norm(pooled[None, :]).astype(jnp.bfloat16)
    feature_rows = t_query.shape[0]
    my_features = lax.dynamic_slice_in_dim(pooled_normed, tok_index * feature_rows, feature_rows, 1)
    query_part = jnp.dot(my_features, t_query, preferred_element_type=jnp.float32)
    key_part = jnp.dot(my_features, t_key, preferred_element_type=jnp.float32)
    value_part = jnp.dot(my_features, t_value, preferred_element_type=jnp.float32)
    query_full, key_full, value_full = lax.psum((query_part, key_part, value_part), "tok")
    local_heads = HEADS // lax.axis_size("tok")
    my_width = local_heads * HD
    head_start = tok_index * my_width
    query_mine = lax.dynamic_slice_in_dim(query_full, head_start, my_width, 1)
    key_mine = lax.dynamic_slice_in_dim(key_full, head_start, my_width, 1)
    value_mine = lax.dynamic_slice_in_dim(value_full, head_start, my_width, 1)
    position = (SPAN + frame_index).astype(jnp.float32)[None]
    tq = rotate(query_mine.reshape(1, local_heads, HD), position).astype(jnp.bfloat16)
    tk = rotate(key_mine.reshape(1, local_heads, HD), position).astype(jnp.bfloat16)
    tv = value_mine.astype(jnp.bfloat16)
    cache_rows = cache_keys.shape[0]
    rotated = rotate(
        cache_keys.astype(jnp.float32).reshape(cache_rows, local_heads, HD),
        cache_pos.astype(jnp.float32),
    ).astype(jnp.bfloat16)
    local_keys = jnp.concatenate(
        [rotated.reshape(cache_rows, local_heads * HD), tk.reshape(1, local_heads * HD)], axis=0
    )
    local_values = jnp.concatenate([cache_values, tv], axis=0)
    rows_each = cache_rows + 1
    scale = HD ** (-0.5)
    query_heads = tq.astype(jnp.float32).reshape(local_heads, HD)
    pieces = (
        lax.all_gather(local_keys, "frame", axis=0, tiled=True),
        lax.all_gather(local_values, "frame", axis=0, tiled=True),
    )
    best = jnp.full((local_heads,), -1e30, jnp.float32)
    count = pieces[0].shape[0]
    index = jnp.arange(count, dtype=jnp.int32)
    owner = index // rows_each
    fresh = index % rows_each == rows_each - 1
    valid = jnp.logical_or(jnp.logical_not(fresh), owner <= frame_index)
    key_heads = pieces[0].astype(jnp.float32).reshape(count, local_heads, HD)
    value_heads = pieces[1].astype(jnp.float32).reshape(count, local_heads, HD)
    scores = jnp.einsum("hd,nhd->hn", query_heads, key_heads) * scale
    scores = jnp.where(valid[None, :], scores, -1e30)
    top = jnp.maximum(best, jnp.max(scores, axis=1))
    weight = jnp.where(valid[None, :], jnp.exp(scores - top[:, None]), 0.0)
    total = jnp.sum(weight, axis=1)
    summed = jnp.einsum("hn,nhd->hd", weight, value_heads)
    best, total, summed = (top, total, summed)
    temporal = (summed / total[:, None]).reshape(1, local_heads * HD).astype(jnp.bfloat16)
    partial_out = jnp.dot(temporal, t_out, preferred_element_type=jnp.float32)
    mixed_heads = lax.psum_scatter(partial_out, "tok", scatter_dimension=1, tiled=True)
    columns = mixed_heads.shape[1]
    pooled_columns = lax.dynamic_slice_in_dim(pooled, tok_index * columns, columns, 0)
    frame_out = (pooled_columns[None, :] + mixed_heads).astype(jnp.bfloat16)
    return (result[None], frame_out)


def solution(mesh):
    return jax.shard_map(
        body,
        mesh=mesh,
        in_specs=(
            P("frame", "tok", None),
            P("tok"),
            P("tok"),
            P("frame", "tok"),
            P("frame", "tok"),
            P("frame", "tok"),
            P("tok", "frame"),
            P("frame", "tok"),
            P("tok", "frame"),
            P("tok", None),
            P("tok", None),
            P("tok", None),
            P("tok", None),
            P("frame", "tok"),
            P("frame", "tok"),
            P("frame"),
        ),
        out_specs=(P("frame", "tok", None), P("frame", "tok")),
        check_vma=False,
    )
```

profile of v0, /device:TPU:1, one launch (start us, length us, event | category | flops | bytes accessed | tf_op | source)
XLA Modules:
  0.0 835.1 jit_solution(10083456377274157456)
XLA Ops:
  11.7 4.9 collective-permute-start
  16.6 1.9 collective-permute-start.1
  19.3 1.7 collective-permute-done
  21.0 6.9 collective-permute-done.1
  27.9 2.1 compare_select_fusion
  30.0 43.9 %all-gather.1 = bf16[32,44,176]{2,1,0:T(8,128)(2,1)S(1)} all-gather(bf16[1,44,176]{2,1,0:T(8,128)(2,1)S(1)} %bitcast.78), channel_id=1, replica_groups=mesh['frame'=32,'tok'=8] {'frame'}, dimensions={0}, use_global_device_ids=true | all-gather | bytes 511104 | tf_op jit(solution)/shard_map/all_gather | solution.py:92
  74.3 57.5 %all-gather = bf16[32,44,176]{2,1,0:T(8,128)(2,1)S(1)} all-gather(bf16[1,44,176]{2,1,0:T(8,128)(2,1)S(1)} %bitcast.79), channel_id=1, replica_groups=mesh['frame'=32,'tok'=8] {'frame'}, dimensions={0}, use_global_device_ids=true | all-gather | bytes 511104 | tf_op jit(solution)/shard_map/all_gather | solution.py:91
  132.9 41.1 %all-gather.2 = bf16[32,44,176]{2,1,0:T(8,128)(2,1)S(1)} all-gather(bf16[1,44,176]{2,1,0:T(8,128)(2,1)S(1)} %bitcast.80), channel_id=1, replica_groups=mesh['frame'=32,'tok'=8] {'frame'}, dimensions={0}, use_global_device_ids=true | all-gather | bytes 511104 | tf_op jit(solution)/shard_map/all_gather | solution.py:93
  174.4 42.5 %all-gather.3 = bf16[32,44,176]{2,1,0:T(8,128)(2,1)S(1)} all-gather(bf16[1,44,176]{2,1,0:T(8,128)(2,1)S(1)} %bitcast.81), channel_id=1, replica_groups=mesh['frame'=32,'tok'=8] {'frame'}, dimensions={0}, use_global_device_ids=true | all-gather | bytes 511104 | tf_op jit(solution)/shard_map/all_gather | solution.py:99
  217.3 3.1 convolution_convert_fusion.3
  227.6 2.6 convolution_convert_fusion
  231.5 102.4 %reduce-scatter.6.cloned.1.call-done = bf16[128,1408]{1,0:T(8,128)(2,1)} async-done(((bf16[1024,1408]{1,0:T(8,128)(2,1)}), bf16[128,1408]{1,0:T(8,128)(2,1)}) %reduce-scatter.6.cloned.1.call-update) | async-done | bytes 360464 | tf_op jit(solution)/shard_map/reduce_scatter | solution.py:102
  336.4 2.6 reshape.263
  339.0 32.9 %all-gather.19.cloned.1.call-done = bf16[32,44,768]{2,1,0:T(8,128)(2,1)} async-done(((bf16[1,44,768]{2,1,0:T(8,128)(2,1)}), bf16[32,44,768]{2,1,0:T(8,128)(2,1)}) %all-gather.19.cloned.1.call-update) | async-done | bytes 2162704 | tf_op jit(solution)/shard_map/all_gather | solution.py:112
  371.9 4.0 reshape.265
  375.8 81.7 %all-gather.15.cloned.1.call-done = bf16[1024,1408]{1,0:T(8,128)(2,1)} async-done(((bf16[128,1408]{1,0:T(8,128)(2,1)}), bf16[1024,1408]{1,0:T(8,128)(2,1)}) %all-gather.15.cloned.1.call-update) | async-done | bytes 2883600 | tf_op jit(solution)/shard_map/all_gather | solution.py:107
  457.6 9.7 %convolution_convert_fusion.1 = bf16[1024,1408]{1,0:T(8,128)(2,1)} fusion(bf16[1408,768]{1,0:T(8,128)(2,1)} %reshape.265, bf16[1024,1408]{1,0:T(8,128)(2,1)} %all-gather.15.cloned.1.call-done, bf16[1408,768]{1,0:T(8,128)(2,1)S(1)} %reshape.263), kind=kOutput, calls=%fused_computation.8 | convolution fusion | flops 4437704704 | bytes 10092544 | tf_op jit(solution)/shard_map/dot_general | solution.py:110
  468.4 103.7 %reduce-scatter.8.cloned.1.call-done = bf16[128,1408]{1,0:T(8,128)(2,1)} async-done(((bf16[1024,1408]{1,0:T(8,128)(2,1)}), bf16[128,1408]{1,0:T(8,128)(2,1)}) %reduce-scatter.8.cloned.1.call-update) | async-done | bytes 360464 | tf_op jit(solution)/shard_map/reduce_scatter | solution.py:115
  572.2 1.8 convert_reduce_fusion.2
  574.0 20.7 %psum.28 = f32[1408]{0:T(1024)S(1)} all-reduce(f32[1408]{0:T(1024)S(1)} %get-tuple-element.11), channel_id=1, replica_groups=mesh['frame'=32,'tok'=8] {'tok'}, use_global_device_ids=true, to_apply=%region_11.12 | all-reduce | flops 1408 | bytes 11264 | tf_op jit(solution)/shard_map/psum | solution.py:121
  597.9 45.3 %all-reduce = (bf16[1,1408]{1,0:T(2,128)(2,1)S(1)}, f32[1,1408]{1,0:T(1,128)S(1)}, f32[1,1408]{1,0:T(1,128)S(1)}) all-reduce(f32[1,1408]{1,0:T(1,128)S(1)} %fusion.80, f32[1,1408]{1,0:T(1,128)S(1)} %fusion.79, f32[1,1408]{1,0:T(1,128)S(1)} %fusion.78), channel_id=1, replica_groups=mesh['frame'=32,'tok'=8] {'tok'}, use_global_device_ids=true, to_apply=%region_17.18 | all-reduce | flops 4224 | bytes 30976 | tf_op jit(solution)/shard_map/psum | solution.py:128
  643.8 58.7 %all-gather.6 = bf16[32,63,176]{2,1,0:T(8,128)(2,1)S(1)} all-gather(bf16[1,63,176]{2,1,0:T(8,128)(2,1)S(1)} %maximum_bitcast_fusion), channel_id=1, replica_groups=mesh['frame'=32,'tok'=8] {'frame'}, dimensions={0}, use_global_device_ids=true | all-gather | bytes 731808 | tf_op jit(solution)/shard_map/all_gather | solution.py:152
  704.1 42.6 %all-gather.7 = bf16[32,63,176]{2,1,0:T(8,128)(2,1)S(1)} all-gather(bf16[1,63,176]{2,1,0:T(8,128)(2,1)S(1)} %maximum_bitcast_fusion.1), channel_id=1, replica_groups=mesh['frame'=32,'tok'=8] {'frame'}, dimensions={0}, use_global_device_ids=true | all-gather | bytes 731808 | tf_op jit(solution)/shard_map/all_gather | solution.py:153
  749.3 77.0 %reduce-scatter.10.cloned.1.call-done = f32[176,1]{1,0:T(8,128)} async-done(((f32[1408,1]{1,0:T(8,128)}), f32[176,1]{1,0:T(8,128)}) %reduce-scatter.10.cloned.1.call-update) | async-done | bytes 720
  (107 shorter events, 26.5 us)
Async XLA Ops:
  8.0 589.4 %copy-start = (bf16[176,1408]{1,0:T(8,128)(2,1)S(1)}, bf16[176,1408]{1,0:T(8,128)(2,1)}, u32[]{:S(2)}) copy-start(bf16[176,1408]{1,0:T(8,128)(2,1)} %param.25) | copy-start | bytes 1486852
  8.0 22.0 %copy-start.9 = (bf16[44,176]{1,0:T(8,128)(2,1)S(1)}, bf16[44,176]{1,0:T(8,128)(2,1)}, u32[]{:S(2)}) copy-start(bf16[44,176]{1,0:T(8,128)(2,1)} %param.20) | copy-start | bytes 46468
  8.0 66.2 %copy-start.10 = (bf16[44,176]{1,0:T(8,128)(2,1)S(1)}, bf16[44,176]{1,0:T(8,128)(2,1)}, u32[]{:S(2)}) copy-start(bf16[44,176]{1,0:T(8,128)(2,1)} %param.19) | copy-start | bytes 46468
  8.0 209.2 %all-gather.13.cloned.1.call-start = ((), (), s32[]{:S(2)}) async-start(), calls=%async_computation.3 | async-start | bytes 3244032 | tf_op jit(solution)/shard_map/all_gather | solution.py:86
  11.7 9.3 %collective-permute-start = (bf16[128,1408]{1,0:T(8,128)(2,1)S(1)}, bf16[128,1408]{1,0:T(8,128)(2,1)S(1)}, u32[]{:S(2)}, u32[]{:S(2)}) collective-permute-start(bf16[128,1408]{1,0:T(8,128)(2,1)S(1)} %fusion.32), channel_id=1, source_target_pairs={{0,8},{8,16},{16,24},{24,32},{32,40},{40,48},{48,56},{56,64},{64,7... | collective-permute-start | bytes 1081352 | tf_op jit(solution)/shard_map/ppermute | solution.py:15
  16.6 11.2 %collective-permute-start.1 = (bf16[128,1408]{1,0:T(8,128)(2,1)S(1)}, bf16[128,1408]{1,0:T(8,128)(2,1)S(1)}, u32[]{:S(2)}, u32[]{:S(2)}) collective-permute-start(bf16[128,1408]{1,0:T(8,128)(2,1)S(1)} %fusion.32), channel_id=1, source_target_pairs={{8,0},{16,8},{24,16},{32,24},{40,32},{48,40},{56,48},{64,56},{72,6... | collective-permute-start | bytes 1081352 | tf_op jit(solution)/shard_map/ppermute | solution.py:15
  27.8 105.1 %copy-start.11 = (bf16[44,176]{1,0:T(8,128)(2,1)S(1)}, bf16[44,176]{1,0:T(8,128)(2,1)}, u32[]{:S(2)}) copy-start(bf16[44,176]{1,0:T(8,128)(2,1)} %param.21) | copy-start | bytes 46468
  30.0 303.9 %reduce-scatter.6.cloned.1.call-start = ((), (), s32[]{:S(2)}) async-start(), calls=%async_computation.4 | async-start | bytes 3244032 | tf_op jit(solution)/shard_map/reduce_scatter | solution.py:102
  73.9 100.4 %copy-start.12 = (bf16[176,44]{0,1:T(8,128)(2,1)S(1)}, bf16[176,44]{0,1:T(8,128)(2,1)}, u32[]{:S(2)}) copy-start(bf16[176,44]{0,1:T(8,128)(2,1)} %param.22) | copy-start | bytes 46468
  217.2 3.2 copy-start.3
  217.3 3.1 copy-start.1
  227.6 106.3 %copy-start.2 = (bf16[1,128,1408]{2,1,0:T(8,128)(2,1)S(1)}, bf16[1,128,1408]{2,1,0:T(8,128)(2,1)}, u32[]{:S(2)}) copy-start(bf16[1,128,1408]{2,1,0:T(8,128)(2,1)} %param.16) | copy-start | bytes 1081348
  230.3 106.1 %all-gather.17.cloned.1.call-start = ((), (), s32[]{:S(2)}) async-start(), calls=%async_computation.7 | async-start | bytes 2433024 | tf_op jit(solution)/shard_map/all_gather | solution.py:108
  230.9 141.0 %all-gather.19.cloned.1.call-start = ((), (), s32[]{:S(2)}) async-start(), calls=%async_computation.8 | async-start | bytes 2433024 | tf_op jit(solution)/shard_map/all_gather | solution.py:112
  231.4 226.1 %all-gather.15.cloned.1.call-start = ((), (), s32[]{:S(2)}) async-start(), calls=%async_computation.5 | async-start | bytes 3244032 | tf_op jit(solution)/shard_map/all_gather | solution.py:107
  336.3 235.8 %reduce-scatter.8.cloned.1.call-start = ((), (), s32[]{:S(2)}) async-start(), calls=%async_computation.6 | async-start | bytes 3244032 | tf_op jit(solution)/shard_map/reduce_scatter | solution.py:115
  375.8 91.7 %copy-start.13 = (s32[62]{0:T(128)S(1)}, s32[62]{0:T(128)}, u32[]{:S(2)}) copy-start(s32[62]{0:T(128)} %param.31) | copy-start | bytes 748
  375.8 91.8 %copy-start.7 = (bf16[62,176]{1,0:T(8,128)(2,1)S(1)}, bf16[62,176]{1,0:T(8,128)(2,1)}, u32[]{:S(2)}) copy-start(bf16[62,176]{1,0:T(8,128)(2,1)} %param.29) | copy-start | bytes 65476
  467.3 130.3 %copy-start.4 = (bf16[176,1408]{1,0:T(8,128)(2,1)S(1)}, bf16[176,1408]{1,0:T(8,128)(2,1)}, u32[]{:S(2)}) copy-start(bf16[176,1408]{1,0:T(8,128)(2,1)} %param.26) | copy-start | bytes 1486852
  467.3 130.4 %copy-start.5 = (bf16[176,1408]{1,0:T(8,128)(2,1)S(1)}, bf16[176,1408]{1,0:T(8,128)(2,1)}, u32[]{:S(2)}) copy-start(bf16[176,1408]{1,0:T(8,128)(2,1)} %param.27) | copy-start | bytes 1486852
  467.3 358.9 %reduce-scatter.10.cloned.1.call-start = ((), (), s32[]{:S(2)}) async-start(), calls=%async_computation.9 | async-start | bytes 811008
  574.0 130.1 %copy-start.8 = (bf16[62,176]{1,0:T(8,128)(2,1)S(1)}, bf16[62,176]{1,0:T(8,128)(2,1)}, u32[]{:S(2)}) copy-start(bf16[62,176]{1,0:T(8,128)(2,1)} %param.30) | copy-start | bytes 65476
  703.1 44.7 %copy-start.6 = (bf16[176,1408]{1,0:T(8,128)(2,1)S(1)}, bf16[176,1408]{1,0:T(8,128)(2,1)}, u32[]{:S(2)}) copy-start(bf16[176,1408]{1,0:T(8,128)(2,1)} %param.28) | copy-start | bytes 1486852
Sparse Core Ops, SparseCore 0:
  30.1 97.3 all-gather.12
  230.4 103.4 reduce-scatter.5
  467.4 104.6 reduce-scatter.7
Sparse Core Ops, SparseCore 1:
  232.6 73.6 all-gather.16
  308.0 63.8 all-gather.18
  374.9 82.6 all-gather.14
  749.3 76.9 reduce-scatter.9
where the time goes:
time: 837 us; the launch traced here: 835 us
  waiting for transfers between devices  407 us (49%)
  blocking collectives  352 us (42%)
  matrix products  23.6 us (3%)
  between operations  17.2 us (2%)
  other arithmetic  15.2 us (2%)
  local copies, waits for them, and re-layouts  11.9 us (1%)
    reduce_scatter x1, waiting for transfers between devices, body(): lax.psum_scatter(down_terms.astype(jnp.bfloat16), 'tok', scatter_dimensio...  104 us
    reduce_scatter x1, waiting for transfers between devices, body(): lax.psum_scatter(projected.astype(jnp.bfloat16), 'tok', scatter_dimension...  102 us
    all_gather x1, waiting for transfers between devices, body(): second_rows = lax.all_gather(second, 'tok', axis=0, tiled=True)  81.7 us
    unnamed x8, waiting for transfers between devices  78.1 us
    all_gather x1, blocking collectives, body(): lax.all_gather(local_keys, 'frame', axis=0, tiled=True)  58.7 us
    all_gather x1, blocking collectives, body(): query = add_one(lax.all_gather(w_query, 'frame', axis=0, tiled=True))  57.5 us
    psum x1, blocking collectives, body(): lax.psum((query_part, key_part, value_part), 'tok')  45.3 us
    all_gather x1, blocking collectives, body(): key = add_one(lax.all_gather(w_key, 'frame', axis=0, tiled=True))  43.9 us
  transfers between devices with their start and end apart: 9, of which 7 were waited for; matrix products, arithmetic and copies ran while one was open for 2% of the time, Pallas kernels for 0%

commit v1 on v0

v1 whole, which is shorter than its diff:
```python
import jax
import jax.numpy as jnp
import numpy as np
from jax import lax
from jax.experimental import pallas as pl
from jax.experimental.pallas import tpu as pltpu
from jax.sharding import PartitionSpec as P

HEADS = 16
HD = 88
P_SIZE = 1024
SPAN = 4096
FRAMES = 32
D = 1408
DP = 1536
QW = 384
TOK = 128
SCALE = HD ** (-0.5)
RATE = SCALE * 1.4426950408889634
MESH = pl.DeviceIdType.MESH
F32 = jnp.float32
BF = jnp.bfloat16
WC = 768
W_ROWS, CACHE_ROWS, CACHE_COLS = 48, 64, 512
WINDOWS = ((0, 384), (256, 512), (640, 512), (1024, 384))


def dot(a, b):
    return jnp.dot(a, b, preferred_element_type=F32)


def dot_nt(a, b):
    return lax.dot_general(a, b, (((1,), (1,)), ((), ())), preferred_element_type=F32)


def iota(shape, axis):
    return lax.broadcasted_iota(jnp.int32, shape, axis)


def mod(a, n):
    return lax.rem(a + n, n)


class Copies:
    def __init__(self, send, recv):
        self.send, self.recv, self.used, self.open = send, recv, 0, []

    def start(self, src, dst, device):
        n = self.used
        self.used += 1
        copy = pltpu.make_async_remote_copy(
            src_ref=src,
            dst_ref=dst,
            send_sem=self.send.at[n],
            recv_sem=self.recv.at[n],
            device_id=device,
            device_id_type=MESH,
        )
        copy.start()
        self.open.append(copy)
        return copy

    def retire(self, keep=0):
        while len(self.open) > keep:
            self.open.pop(0).wait_send()


def norm_padded(v, valid):
    mean = jnp.sum(v, axis=1, keepdims=True) * (1.0 / D)
    center = jnp.where(valid, v - mean, 0.0)
    spread = jnp.sum(center * center, axis=1, keepdims=True) * (1.0 / D)
    return center * lax.rsqrt(spread + 1e-06)


def as_column(row):
    spread = jnp.where(iota((TOK, TOK), 0) == iota((TOK, TOK), 1), row, 0.0)
    return jnp.sum(spread, axis=1, keepdims=True)


def kernel(
    patches_hbm, offset_hbm, piece_hbm, wq_hbm, wk_hbm, wv_hbm, wo_hbm, wu_hbm, wd_hbm,
    tq_hbm, tk_hbm, tv_hbm, to_hbm, ck_hbm, cv_hbm, pos_hbm, table_hbm, turn_hbm,
    out, frame_out,
    patches, offset_in, piece_in, wq, wk, wv, wo, wu, wd, tq_w, tk_w, tv_w, to_w, ck_in, cv_in, pos_in, table, turn,
    meta, xin, meta_in, src, src_in, pad, res, WA, WU, WU2, WD, WD2, C, comp, around, H1, KV, Q,
    SB, RB, RC, mixed, H2, HID, SB2, RB2, RC2,
    result, swapped, sums, pooled, qkv_send, qkv_recv, new_send, new_all, last_send, last_recv,
    local, big_send, big_recv, swap_send, swap_recv, s1, r1, s2, r2, s3, r3, s4, r4,
):
    f = lax.axis_index("frame")
    t = lax.axis_index("tok")
    x, zl, c = lax.div(f, 8), lax.div(lax.rem(f, 8), 2), lax.rem(f, 2)
    y, zh = lax.div(t, 2), lax.rem(t, 2)
    z = zh * 4 + zl

    def place(r):
        return (r + 2) % 8

    loads = [
        pltpu.make_async_copy(a, b, local.at[n])
        for n, (a, b) in enumerate(
            (
                (patches_hbm, patches), (offset_hbm, offset_in), (piece_hbm, piece_in),
                (wq_hbm, wq), (wk_hbm, wk), (wv_hbm, wv), (wo_hbm, wo), (wu_hbm, wu), (wd_hbm, wd),
                (ck_hbm, ck_in), (cv_hbm, cv_in), (pos_hbm, pos_in), (table_hbm, table),
                (turn_hbm.at[f], turn), (tq_hbm, tq_w), (tk_hbm, tk_w), (tv_hbm, tv_w), (to_hbm, to_w),
            )
        )
    ]
    for load in loads:
        load.start()
    new_all[...] = jnp.zeros_like(new_all)

    def dev(x_at, z_at, y_at, c_at):
        return (x_at * 8 + lax.rem(z_at, 4) * 2 + c_at, y_at * 2 + lax.div(z_at, 4))

    xp, xm = dev(mod(x + 1, 4), z, y, c), dev(mod(x - 1, 4), z, y, c)
    yp, ym = dev(x, z, mod(y + 1, 4), c), dev(x, z, mod(y - 1, 4), c)
    zp, zm = dev(x, mod(z + 1, 8), y, c), dev(x, mod(z - 1, 8), y, c)
    sibling = dev(x, z, y, 1 - c)
    partner = dev(x, mod(z + 4, 8), y, 1 - c)
    after, before = (mod(f + 1, 32), t), (mod(f - 1, 32), t)

    barrier = pltpu.get_barrier_semaphore()
    friends = (xp, xm, yp, ym, zp, zm, sibling, partner, after, before)
    for friend in friends:
        pl.semaphore_signal(barrier, inc=1, device_id=friend, device_id_type=MESH)
    pl.semaphore_wait(barrier, len(friends))

    copies = Copies(big_send, big_recv)
    moves = c != zh

    def remote(src, dst, send, recv, device):
        return pltpu.make_async_remote_copy(
            src_ref=src, dst_ref=dst, send_sem=send, recv_sem=recv,
            device_id=device, device_id_type=MESH,
        )

    def swap(src, dst, n):
        return remote(src, dst, swap_send.at[n], swap_recv.at[n], partner)

    for load in loads[0:3]:
        load.wait()
    meta[0:1, :] = offset_in[...].astype(F32)
    meta[1:2, :] = piece_in[...].astype(F32)

    @pl.when(moves)
    def _():
        swap(patches, xin, 0).start()
        swap(meta, meta_in, 1).start()

    @pl.when(jnp.logical_not(moves))
    def _():
        xin[...] = patches[...]
        meta_in[...] = meta[...]

    for load in loads[3:7]:
        load.wait()
    grow = jnp.where(iota((48, 44), 0) == iota((48, 44), 1), 1.0, 0.0).astype(BF)
    total = None
    for n, w in enumerate((wq, wk, wv, wo)):
        to = jnp.where(
            iota((176, WC), 0) + n * 176 == iota((176, WC), 1), 1.0, 0.0
        ).astype(BF)
        term = dot(dot(grow, w[...]).astype(BF), to)
        total = term if total is None else total + term
    WA[0, 0, place(0)] = total.astype(BF)

    def z_first(B):
        def at(r):
            return B.at[0, 0, place(r)]

        waits = [copies.start(at(0), at(-1), zp), copies.start(at(0), at(1), zm)]
        yield
        firsts = []

        def across(run):
            firsts.append(copies.start(B.at[0, 0, run], B.at[0, 3, run], xp))
            firsts.append(copies.start(B.at[0, 0, run], B.at[0, 1, run], xm))

        half = B.shape[4] // 2
        low, high = pl.ds(0, half), pl.ds(half, half)
        for step in range(1, 5):
            for copy in waits:
                copy.wait_recv()
            if step < 3:
                waits = [
                    copies.start(at(-step), at(-step - 1), zp),
                    copies.start(at(step), at(step + 1), zm),
                ]
            elif step == 3:
                waits = [
                    copies.start(B.at[0, 0, place(-3), :, low], B.at[0, 0, place(4), :, low], zp),
                    copies.start(B.at[0, 0, place(3), :, high], B.at[0, 0, place(4), :, high], zm),
                ]
            if step == 2:
                across(pl.ds(0, 5))
            if step == 4:
                across(pl.ds(5, 3))
            if step < 4:
                yield

        def aside(x_at):
            return copies.start(B.at[0, x_at], B.at[1, x_at], sibling)

        sides = [aside(0)]
        yield
        for copy in firsts:
            copy.wait_recv()
        one, two = pl.ds(0, 4), pl.ds(4, 4)
        waits = [
            copies.start(B.at[0, 3, one], B.at[0, 2, one], xp),
            copies.start(B.at[0, 1, two], B.at[0, 2, two], xm),
        ]
        sides += [aside(3), aside(1)]
        yield
        for copy in waits:
            copy.wait_recv()
        sides.append(aside(2))
        yield
        for copy in sides:
            copy.wait_recv()

    def x_first(B):
        here = place(0)
        waits = [
            copies.start(B.at[0, here, 0], B.at[0, here, 3], xp),
            copies.start(B.at[0, here, 0], B.at[0, here, 1], xm),
        ]
        yield
        half = B.shape[4] // 2
        low, high = pl.ds(0, half), pl.ds(half, half)
        for copy in waits:
            copy.wait_recv()
        waits = [
            copies.start(B.at[0, here, 3, :, low], B.at[0, here, 2, :, low], xp),
            copies.start(B.at[0, here, 1, :, high], B.at[0, here, 2, :, high], xm),
        ]
        yield

        def at(r):
            return B.at[0, place(r)]

        one, two = pl.ds(0, 2), pl.ds(2, 2)
        for step in range(5):
            for copy in waits:
                copy.wait_recv()
            if step < 3:
                waits = [
                    copies.start(at(-step), at(-step - 1), zp),
                    copies.start(at(step), at(step + 1), zm),
                ]
                yield
            elif step == 3:
                waits = [
                    copies.start(B.at[0, place(-3), one], B.at[0, place(4), one], zp),
                    copies.start(B.at[0, place(3), two], B.at[0, place(4), two], zm),
                ]
                yield
        side = copies.start(B.at[0], B.at[1], sibling)
        yield
        side.wait_recv()

    def drain(task):
        for _ in task:
            pass

    def ahead(task, count):
        for _ in range(count):
            if next(task, "end") == "end":
                return

    def both(*tasks):
        tasks = list(tasks)
        while tasks:
            for task in list(tasks):
                if next(task, "end") == "end":
                    tasks.remove(task)
            if tasks:
                yield

    load1, load4 = z_first(WA), x_first(C)
    load2 = both(z_first(WU), x_first(WU2))
    load3 = both(z_first(WD), x_first(WD2))
    ahead(load1, 1)

    for q, (start, size) in enumerate(WINDOWS):
        r, k = iota((size, QW), 0) + start, iota((size, QW), 1)
        at = lax.rem(k, 48)
        hit = (r == 352 * q + lax.div(k, 48) * 44 + at) & (at < 44)
        pad[q, 0:size, :] = jnp.where(hit, 1.0, 0.0).astype(BF)
    valid = lax.rem(iota((1, DP), 1), 48) < 44

    def padded(rows):
        for q, (start, size) in enumerate(WINDOWS):
            res[:, q * QW : (q + 1) * QW] = dot(
                rows[:, start : start + size], pad[q, 0:size, :]
            ).astype(BF)
        normed = norm_padded(res[...].astype(F32), valid)
        return [normed[:, q * QW : (q + 1) * QW] for q in range(4)]

    quarters = padded(patches)
    offset, piece = as_column(meta[0:1, :]), as_column(meta[1:2, :])
    mine = quarters[0]
    for q in range(1, 4):
        mine = jnp.where(piece == float(q), quarters[q], mine)
    comp[...] = mine.astype(BF)
    hops = [
        copies.start(comp, around.at[0], after),
        copies.start(comp, around.at[1], before),
    ]
    for load in loads[7:9]:
        load.wait()
    for w, one, two in ((wu, WU, WU2), (wd, WD, WD2)):
        rows = dot(grow, w[...]).astype(BF)
        one[0, 0, place(0)] = rows[:, 0:512]
        two[0, place(0), 0] = rows[:, 512:768]
    ahead(load1, 1)
    for copy in hops:
        copy.wait_recv()
    earlier = jnp.where(f > 0, around[0].astype(F32), 0.0)
    later = jnp.where(f < FRAMES - 1, around[1].astype(F32), 0.0)
    source = jnp.where(
        offset == -1.0, earlier, jnp.where(offset == 1.0, later, comp[...].astype(F32))
    )
    src[...] = source.astype(BF)

    @pl.when(moves)
    def _():
        swap(src, src_in, 2).start()

    @pl.when(jnp.logical_not(moves))
    def _():
        src_in[...] = src[...]

    ahead(load1, 1)

    def turned(v):
        return jnp.concatenate([v[:, 44:88], v[:, 0:44], v[:, 132:176], v[:, 88:132]], axis=1)

    for load in loads[9:13]:
        load.wait()
    spot = jnp.where(
        iota((CACHE_ROWS, 62), 0) == iota((CACHE_ROWS, 62), 1), pos_in[...].astype(F32), 0.0
    )
    spot = jnp.sum(spot, axis=1, keepdims=True)
    high = jnp.floor(spot * (1.0 / 64))
    lanes = iota((CACHE_ROWS, 64), 1).astype(F32)

    def chosen(at, n):
        hit = jnp.where(lanes == at, 1.0, 0.0)
        both = jnp.dot(hit, table[n], preferred_element_type=F32, precision=lax.Precision.HIGHEST)
        return both[0:62, 0:176], both[0:62, 176:352]

    (cos_a, sin_a), (cos_b, sin_b) = chosen(high, 0), chosen(spot - 64.0 * high, 1)
    cosine, sine = cos_a * cos_b - sin_a * sin_b, sin_a * cos_b + cos_a * sin_b
    sine = jnp.where(lax.rem(iota((62, 176), 1), HD) < HD // 2, -sine, sine)
    raw = ck_in[...].astype(F32)
    C[0, place(0), 0] = jnp.zeros((CACHE_ROWS, CACHE_COLS), BF)
    C[0, place(0), 0, 0:62, 0:176] = (raw * cosine + turned(raw) * sine).astype(BF)
    C[0, place(0), 0, 0:62, 256:432] = cv_in[...]
    ahead(load1, 2)

    @pl.when(moves)
    def _():
        swap(patches, xin, 0).wait()
        swap(meta, meta_in, 1).wait()
        swap(src, src_in, 2).wait()

    quarters = padded(xin)
    piece = as_column(meta_in[1:2, :])
    for q in range(4):
        H1[0, :, q * QW : (q + 1) * QW] = jnp.where(
            piece == float(q), src_in[...].astype(F32), quarters[q]
        ).astype(BF)

    def gather(H):
        a, b = pl.ds(0, 64), pl.ds(64, 64)
        one = copies.start(H.at[0, a], H.at[3, a], yp)
        two = copies.start(H.at[0, b], H.at[1, b], ym)
        rest = [
            copies.start(H.at[0, b], H.at[3, b], yp), copies.start(H.at[0, a], H.at[1, a], ym)
        ]
        yield
        one.wait_recv()
        far = [copies.start(H.at[3, a], H.at[2, a], yp)]
        two.wait_recv()
        far.append(copies.start(H.at[1, b], H.at[2, b], ym))
        yield
        for copy in rest:
            copy.wait_recv()
        yield
        for copy in far:
            copy.wait_recv()

    rows1 = gather(H1)
    ahead(rows1, 1)
    ahead(load2, 2)
    ahead(rows1, 1)
    ahead(load1, 1)
    ahead(load2, 1)
    ahead(rows1, 1)
    ahead(load2, 1)
    drain(rows1)
    ahead(load1, 1)
    drain(load1)
    ahead(load2, 1)

    plane_of = [c, 1 - c]
    x_of = [mod(k - x, 4) for k in range(4)]
    z_of = [lax.rem(k - z + 8 + 2, 8) for k in range(8)]

    def weight(B, at, start, size):
        pieces = []
        for k in range(32):
            p, x_at, z_at = plane_of[k % 2], x_of[k // 8], z_of[at * 4 + k // 2 % 4]
            spot = (p, x_at, z_at) if B.shape[1] == 4 else (p, z_at, x_at)
            pieces.append(B[(*spot, slice(None), slice(start, start + size))])
        return jnp.concatenate(pieces, axis=0)

    def wider(rows, first, columns, start):
        r, k = iota((rows, columns), 0) + first, iota((rows, columns), 1) + start
        at = lax.rem(k, 128)
        return jnp.where((r == lax.div(k, 128) * HD + at) & (at < HD), 1.0, 0.0).astype(BF)

    wide_q, wide_kv = wider(256, 0, 256, 0), wider(512, 128, 512, 256)
    r, k = iota((256, 256), 1) + 512, iota((256, 256), 0)
    at = lax.rem(k, 128)
    narrow = jnp.where(
        (r == 528 + lax.div(k, 128) * HD + at) & (at < HD), 1.0, 0.0
    ).astype(BF)

    rows = H1[...].reshape(4 * TOK, DP)
    sides = []
    for at in range(2):
        joined = dot(rows, weight(WA, at, 128, 512)).astype(BF)
        KV[0, at] = dot(joined, wide_kv).astype(BF)
        sides.append(copies.start(KV.at[0, at], KV.at[1, at], sibling))
    ahead(load3, 1)
    for at in range(2):
        joined = dot(rows, weight(WA, at, 0, 256)).astype(BF)
        Q[at] = dot(joined, wide_q).astype(BF).reshape(4, TOK, 256)
    ahead(load3, 1)
    for copy in sides:
        copy.wait_recv()

    def attend(block):
        total = None
        for at in range(2):
            heads = []
            for h in range(2):
                span = slice(h * 128, h * 128 + 128)
                vspan = slice(256 + h * 128, 256 + h * 128 + 128)
                q = Q[at, block, :, span]
                s = [dot_nt(q, KV[k, at, :, span]) for k in range(2)]
                top = jnp.maximum(
                    jnp.max(s[0], axis=1, keepdims=True), jnp.max(s[1], axis=1, keepdims=True)
                )
                p = [jnp.exp2(part * RATE - top * RATE) for part in s]
                mass = jnp.sum(p[0], axis=1, keepdims=True) + jnp.sum(p[1], axis=1, keepdims=True)
                o = dot(p[0].astype(BF), KV[0, at, :, vspan]) + dot(
                    p[1].astype(BF), KV[1, at, :, vspan]
                )
                heads.append((o / mass).astype(BF))
            both_heads = dot(jnp.concatenate(heads, axis=1), narrow).astype(BF)
            term = dot_nt(both_heads, weight(WA, at, 512, 256))
            total = term if total is None else total + term
        return total

    def scatter(partial, S, B, R, far_first, between):
        a, b = pl.ds(0, 64), pl.ds(64, 64)

        def send_far():
            S[0] = partial(2).astype(BF)
            return [
                copies.start(S.at[0, a], B.at[0], yp), copies.start(S.at[0, b], B.at[1], ym)
            ]

        def send_near():
            S[1] = partial(1).astype(BF)
            one = copies.start(S.at[1, b], R.at[0, b], yp)
            S[2] = partial(3).astype(BF)
            return [one, copies.start(S.at[2, a], R.at[1, a], ym)]

        if far_first:
            far = send_far()
            between(0)
            near = send_near()
            between(1)
        else:
            near = send_near()
            far = send_far()
            between(0)
        far[0].wait_recv()
        S[1, 0:64, :] = (S[1, 0:64, :].astype(F32) + B[0].astype(F32)).astype(BF)
        near.append(copies.start(S.at[1, a], R.at[0, a], yp))
        far[1].wait_recv()
        S[2, 64:128, :] = (S[2, 64:128, :].astype(F32) + B[1].astype(F32)).astype(BF)
        near.append(copies.start(S.at[2, b], R.at[1, b], ym))
        own = partial(0)
        between(2)
        for copy in near:
            copy.wait_recv()
        return own + R[0].astype(F32) + R[1].astype(F32)

    def beside_attention(n):
        if n == 0:
            ahead(load2, 1)
            ahead(load3, 1)
            ahead(load4, 1)
        elif n == 1:
            ahead(load3, 1)
            ahead(load2, 1)
            ahead(load4, 1)
        else:
            ahead(load3, 1)
            drain(load2)

    total = scatter(attend, SB, RB, RC, True, beside_attention)
    mixed[...] = (res[...].astype(F32) + total).astype(BF)
    H2[0] = norm_padded(mixed[...].astype(F32), valid).astype(BF)
    rows2 = gather(H2)
    ahead(rows2, 1)
    ahead(load3, 1)
    ahead(load4, 1)

    def up(block, at):
        rows = H2[block]
        return [
            jax.nn.gelu(dot(rows, weight(WU, at, 0, 512))).astype(BF),
            jax.nn.gelu(dot(rows, weight(WU2, at, 0, 256))).astype(BF),
        ]

    def down(hidden, at):
        return dot_nt(hidden[0], weight(WD, at, 0, 512)) + dot_nt(
            hidden[1], weight(WD2, at, 0, 256)
        )

    def up_down(block):
        return down(up(block, 0), 0) + down(up(block, 1), 1)

    for at in range(2):
        first, second = up(0, at)
        HID[at, :, 0:512] = first
        HID[at, :, 512:768] = second
    ahead(rows2, 1)
    copies.retire(24)
    ahead(load4, 1)
    ahead(rows2, 1)
    ahead(load3, 1)
    drain(load3)

    def near_rows(block):
        return up_down(block)

    def far_rows(block):
        ahead(load4, 1)
        drain(rows2)
        return up_down(block)

    def own_rows(block):
        own = [(HID[at, :, 0:512], HID[at, :, 512:768]) for at in range(2)]
        return down(own[0], 0) + down(own[1], 1)

    def beside_mlp(n):
        if n == 0:
            ahead(load4, 1)
        else:
            ahead(load4, 1)
            copies.retire(8)

    calls = [near_rows, near_rows, far_rows, own_rows]
    total = scatter(lambda block: calls.pop(0)(block), SB2, RB2, RC2, False, beside_mlp)
    last = (mixed[...].astype(F32) + total).astype(BF)
    columns = [
        dot_nt(last[:, q * QW : (q + 1) * QW], pad[q, 0:size, :])
        for q, (_, size) in enumerate(WINDOWS)
    ]
    parts = [
        columns[0][:, 0:256],
        columns[0][:, 256:384] + columns[1][:, 0:128],
        columns[1][:, 128:384],
        columns[1][:, 384:512] + columns[2][:, 0:128],
        columns[2][:, 128:384],
        columns[2][:, 384:512] + columns[3][:, 0:128],
        columns[3][:, 128:384],
    ]
    plain = jnp.concatenate(parts, axis=1)
    sums[...] = jnp.sum(plain, axis=0, keepdims=True)

    other = f + 1 - 2 * c
    home = f - c + zh
    slot = 2 * y + c

    def share(k):
        return remote(sums, pooled.at[slot], s1, r1, (home, lax.rem(t + k, 8)))

    def all_of(ref, send, recv):
        return remote(ref, ref, send, recv, sibling)

    @pl.when(moves)
    def _():
        share(0).start()

    @pl.when(jnp.logical_not(moves))
    def _():
        pooled[slot] = sums[...]

    for k in range(1, 8):
        share(k).start()

    result[...] = plain.astype(BF)

    @pl.when(moves)
    def _():
        swap(result, swapped, 3).start()

    drain(load4)
    for load in loads[13:]:
        load.wait()

    @pl.when(moves)
    def _():
        all_of(pooled, s1, r1).wait_recv()

    @pl.when(jnp.logical_not(moves))
    def _():
        all_of(pooled.at[pl.ds(0, 7)], s1, r1).wait_recv()

    mean_frame = pooled[0]
    for k in range(1, 8):
        mean_frame = mean_frame + pooled[k]
    mean_frame = mean_frame * (1.0 / P_SIZE)
    center = mean_frame - jnp.sum(mean_frame, axis=1, keepdims=True) * (1.0 / D)
    spread = jnp.sum(center * center, axis=1, keepdims=True) * (1.0 / D)
    normed = center * lax.rsqrt(spread + 1e-06)

    def pick(v):
        got = v[:, 0:176]
        for k in range(1, 8):
            got = jnp.where(t == k, v[:, k * 176 : k * 176 + 176], got)
        return got

    features = jnp.broadcast_to(pick(normed), (8, 176)).astype(BF)
    for n, w in enumerate((tq_w, tk_w, tv_w)):
        part = dot(features, w[...])
        for k in range(8):
            qkv_send[k, n, :, 0:176] = part[0:1, k * 176 : k * 176 + 176]

    def send_heads(k):
        to = lax.rem(t + k, 8)
        return remote(qkv_send.at[to], qkv_recv.at[t], s2, r2, (f, to))

    for k in range(1, 8):
        send_heads(k).start()
    qkv_recv[t] = qkv_send[t]
    all_of(qkv_recv.at[pl.ds(0, 7)], s2, r2).wait_recv()

    whole = []
    for n in range(3):
        v = qkv_recv[0, n, :, 0:176]
        for k in range(1, 8):
            v = v + qkv_recv[k, n, :, 0:176]
        whole.append(v)

    def rot(v):
        return (v * turn[0:1, :] + turned(v) * turn[1:2, :]).astype(BF).astype(F32)

    new_send[...] = jnp.zeros_like(new_send)
    new_send[:, 0:176] = rot(whole[1])
    new_send[:, 256:432] = whole[2].astype(BF).astype(F32)


    @pl.loop(1, 32)
    def _(k):
        remote(new_send, new_all.at[f], s3, r3, (lax.rem(f + k, 32), t)).start()

    new_all[f] = new_send[...]
    query = rot(whole[0])
    lane = iota((1, 176), 1)
    wide_query = jnp.concatenate(
        [jnp.where(lane < HD, query, 0.0), jnp.where(lane >= HD, query, 0.0), jnp.zeros((6, 176), F32)],
        axis=0,
    )
    queries = jnp.concatenate([wide_query, jnp.zeros((8, 80), F32)], axis=1).astype(BF)
    count = 32 * CACHE_ROWS
    cached = [C[:, lax.rem(k - zl + 8 + 2, 8)] for k in range(4)]
    old_keys = jnp.concatenate([part[..., 0:256].reshape(-1, 256) for part in cached], axis=0)
    s_old = dot_nt(queries, old_keys)
    s_old = jnp.where(lax.rem(iota((8, count), 1), CACHE_ROWS) < 62, s_old, -1e30)

    all_of(new_all.at[pl.ds(0, 31)], s3, r3).wait_recv()
    known = new_all[:, 0, :]
    s_new = dot_nt(queries, known[:, 0:256].astype(BF))
    s_new = jnp.where(iota((8, 32), 1) <= f, s_new, -1e30)
    top = jnp.maximum(
        jnp.max(s_old, axis=1, keepdims=True), jnp.max(s_new, axis=1, keepdims=True)
    )
    p_old = jnp.exp2(s_old * RATE - top * RATE)
    p_new = jnp.exp2(s_new * RATE - top * RATE)
    p_old = jnp.where(lax.rem(iota((8, count), 1), CACHE_ROWS) < 62, p_old, 0.0)
    p_new = jnp.where(iota((8, 32), 1) <= f, p_new, 0.0)
    mass = jnp.sum(p_old, axis=1, keepdims=True) + jnp.sum(p_new, axis=1, keepdims=True)
    old_values = jnp.concatenate([part[..., 256:512].reshape(-1, 256) for part in cached], axis=0)
    o = dot(p_old.astype(BF), old_values) + dot(p_new.astype(BF), known[:, 256:512].astype(BF))
    o = o / mass
    temporal = jnp.where(lane < HD, o[0:1, 0:176], o[1:2, 0:176])
    part = dot(jnp.broadcast_to(temporal, (8, 176)).astype(BF), to_w[...])
    for k in range(8):
        last_send[k, :, 0:176] = part[0:1, k * 176 : k * 176 + 176]

    def send_last(k):
        to = lax.rem(t + k, 8)
        return remote(last_send.at[to], last_recv.at[t], s4, r4, (f, to))

    for k in range(1, 8):
        send_last(k).start()
    last_recv[t] = last_send[t]

    stored, kept = (pltpu.make_async_copy(a, out, local.at[0]) for a in (swapped, result))

    @pl.when(moves)
    def _():
        swap(result, swapped, 3).wait()
        stored.start()

    @pl.when(jnp.logical_not(moves))
    def _():
        kept.start()

    copies.retire()

    @pl.when(moves)
    def _():
        all_of(pooled, s1, r1).wait_send()

    @pl.when(jnp.logical_not(moves))
    def _():
        all_of(pooled.at[pl.ds(0, 7)], s1, r1).wait_send()

    all_of(qkv_recv.at[pl.ds(0, 7)], s2, r2).wait_send()
    all_of(new_all.at[pl.ds(0, 31)], s3, r3).wait_send()
    all_of(last_recv.at[pl.ds(0, 7)], s4, r4).wait_recv()
    total = pick(mean_frame)
    for k in range(8):
        total = total + last_recv[k, :, 0:176]
    frame_out[...] = total.astype(BF)
    all_of(last_recv.at[pl.ds(0, 7)], s4, r4).wait_send()

    @pl.when(moves)
    def _():
        stored.wait()

    @pl.when(jnp.logical_not(moves))
    def _():
        kept.wait()


BIG = 160


def call(*operands):
    turn = operands[-1]
    vmem = pl.BlockSpec(memory_space=pltpu.VMEM)
    dma = pltpu.SemaphoreType.DMA
    held = [pltpu.VMEM(a.shape, a.dtype) for a in operands[:-1]] + [
        pltpu.VMEM(turn.shape[1:], F32)
    ]
    return pl.pallas_call(
        kernel,
        out_shape=(
            jax.ShapeDtypeStruct((TOK, D), BF),
            jax.ShapeDtypeStruct((1, 176), BF),
        ),
        in_specs=[pl.BlockSpec(memory_space=pl.ANY)] * len(operands),
        out_specs=(pl.BlockSpec(memory_space=pl.ANY), vmem),
        scratch_shapes=held
        + [
            pltpu.VMEM((2, TOK), F32),
            pltpu.VMEM((TOK, D), BF),
            pltpu.VMEM((2, TOK), F32),
            pltpu.VMEM((TOK, QW), BF),
            pltpu.VMEM((TOK, QW), BF),
            pltpu.VMEM((4, 512, QW), BF),
            pltpu.VMEM((TOK, DP), BF),
            pltpu.VMEM((2, 4, 8, W_ROWS, WC), BF),
            pltpu.VMEM((2, 4, 8, W_ROWS, 512), BF),
            pltpu.VMEM((2, 8, 4, W_ROWS, 256), BF),
            pltpu.VMEM((2, 4, 8, W_ROWS, 512), BF),
            pltpu.VMEM((2, 8, 4, W_ROWS, 256), BF),
            pltpu.VMEM((2, 8, 4, CACHE_ROWS, CACHE_COLS), BF),
            pltpu.VMEM((TOK, QW), BF),
            pltpu.VMEM((2, TOK, QW), BF),
            pltpu.VMEM((4, TOK, DP), BF),
            pltpu.VMEM((2, 2, 4 * TOK, 512), BF),
            pltpu.VMEM((2, 4, TOK, 256), BF),
            pltpu.VMEM((3, TOK, DP), BF),
            pltpu.VMEM((2, 64, DP), BF),
            pltpu.VMEM((2, TOK, DP), BF),
            pltpu.VMEM((TOK, DP), BF),
            pltpu.VMEM((4, TOK, DP), BF),
            pltpu.VMEM((2, TOK, 768), BF),
            pltpu.VMEM((3, TOK, DP), BF),
            pltpu.VMEM((2, 64, DP), BF),
            pltpu.VMEM((2, TOK, DP), BF),
            pltpu.VMEM((TOK, D), BF),
            pltpu.VMEM((TOK, D), BF),
            pltpu.VMEM((1, D), F32),
            pltpu.VMEM((8, 1, D), F32),
            pltpu.VMEM((8, 3, 1, 256), F32),
            pltpu.VMEM((8, 3, 1, 256), F32),
            pltpu.VMEM((1, CACHE_COLS), F32),
            pltpu.VMEM((32, 1, CACHE_COLS), F32),
            pltpu.VMEM((8, 1, 256), F32),
            pltpu.VMEM((8, 1, 256), F32),
            dma((len(operands),)),
            dma((BIG,)), dma((BIG,)),
            dma((4,)), dma((4,)),
            dma, dma, dma, dma, dma, dma, dma, dma,
        ],
        compiler_params=pltpu.CompilerParams(
            collective_id=0, has_side_effects=True, vmem_limit_bytes=56 * 1024 * 1024
        ),
        cost_estimate=pl.CostEstimate(
            flops=8_000_000_000, bytes_accessed=20_000_000, transcendentals=3_000_000
        ),
    )(*operands)


def body(
    patches, shift_offset, shift_slice, w_query, w_key, w_value, w_out, w_up, w_down,
    t_query, t_key, t_value, t_out, cache_keys, cache_values, cache_pos,
):
    half = HD // 2
    freq = np.float32(10000.0) ** (-np.arange(half, dtype=np.float32) / np.float32(half))
    angle = (SPAN + np.arange(FRAMES)).astype(np.float32)[:, None] * freq[None, :]
    cosine, sine = np.cos(angle), np.sin(angle)
    turn = np.stack(
        [
            np.concatenate([cosine] * 4, axis=1),
            np.concatenate([-sine, sine, -sine, sine], axis=1),
        ],
        axis=1,
    ).astype(np.float32)
    steps = np.arange(64)[:, None] * (10000.0 ** (-np.arange(half) / half))[None, :]
    table = np.stack(
        [
            np.concatenate([np.cos(64 * steps)] * 4 + [np.sin(64 * steps)] * 4, axis=1),
            np.concatenate([np.cos(steps)] * 4 + [np.sin(steps)] * 4, axis=1),
        ]
    ).astype(np.float32)
    patch_out, frame_out = call(
        patches[0], shift_offset[None], shift_slice[None], w_query, w_key, w_value,
        w_out.T, w_up, w_down.T, t_query, t_key, t_value, t_out, cache_keys, cache_values, cache_pos[None],
        jnp.asarray(table), jnp.asarray(turn),
    )
    return (patch_out[None], frame_out)


def solution(mesh):
    return jax.shard_map(
        body,
        mesh=mesh,
        in_specs=(
            P("frame", "tok", None),
            P("tok"),
            P("tok"),
            P("frame", "tok"),
            P("frame", "tok"),
            P("frame", "tok"),
            P("tok", "frame"),
            P("frame", "tok"),
            P("tok", "frame"),
            P("tok", None),
            P("tok", None),
            P("tok", None),
            P("tok", None),
            P("frame", "tok"),
            P("frame", "tok"),
            P("frame"),
        ),
        out_specs=(P("frame", "tok", None), P("frame", "tok")),
        check_vma=False,
    )
```

time: 837 us -> 149 us (0.18)
  waiting for transfers between devices: 407 us -> 0 us
  blocking collectives: 352 us -> 0 us
  Pallas kernels: 0 us -> 146 us
  matrix products: 23.6 us -> 0 us
  between operations: 17.2 us -> 0.65 us
  other arithmetic: 15.2 us -> 0 us
  local copies, waits for them, and re-layouts: 11.9 us -> 2.31 us
    all_gather x6 -> x0, blocking collectives: 286 us -> none  [the longest x1 58.7 us: body(): lax.all_gather(local_keys, 'frame', axis=0, tiled=True)]
    reduce_scatter x2 -> x0, waiting for transfers between devices: 206 us -> none  [the longest x1 104 us: body(): lax.psum_scatter(down_terms.astype(jnp.bfloat16), 'tok', scatter_dimensio...]
    pallas_call x0 -> x1, Pallas kernels: none -> 146 us  [call(): pl.pallas_call(kernel, out_shape=(jax.ShapeDtypeStruct((TOK, D), BF), jax...]
    all_gather x4 -> x0, waiting for transfers between devices: 115 us -> none  [the longest x1 81.7 us: body(): second_rows = lax.all_gather(second, 'tok', axis=0, tiled=True)]
    unnamed x8 -> x0, waiting for transfers between devices: 78.1 us -> none
    psum x2 -> x0, blocking collectives: 66 us -> none  [the longest x1 45.3 us: body(): lax.psum((query_part, key_part, value_part), 'tok')]
    dot_general x14 -> x0, matrix products: 22.3 us -> none  [the longest x1 9.7 us: body(): jnp.dot(hidden, lax.all_gather(w_down, 'frame', axis=1, tiled=True), pref...]
    ppermute x2 -> x0, waiting for transfers between devices: 8.6 us -> none  [from_behind(): return lax.ppermute(block, axis, route)]
  transfers between devices with their start and end apart: 9 -> 0, of which waited for: 7 -> 0; matrix products, arithmetic and copies ran while one was open for 2% -> 0% of each run, Pallas kernels for 0% -> 0%
where the time goes in v1:
time: 149 us
  Pallas kernels  146 us (98%)
  local copies, waits for them, and re-layouts  2.31 us (2%)
    pallas_call x1, Pallas kernels, call(): pl.pallas_call(kernel, out_shape=(jax.ShapeDtypeStruct((TOK, D), BF), jax...  146 us

profile of v1, /device:TPU:1, one launch (start us, length us, event | category | flops | bytes accessed | tf_op | source)
XLA Modules:
  0.0 149.3 jit_solution(5030225968794878786)
XLA Ops:
  0.6 146.4 %shard_map.185 = (bf16[128,1408]{1,0:T(8,128)(2,1)}, bf16[1,176]{1,0:T(2,128)(2,1)}) custom-call(bf16[128,1408]{1,0:T(8,128)(2,1)} %bitcast.8, s32[1,128]{1,0:T(1,128)} %bitcast.11, s32[1,128]{1,0:T(1,128)} %bitcast.12, bf16[44,176]{1,0:T(8,128)(2,1)} %wq_hbm.1, bf16[44,176]{1,0:T(8,128)(2,1)} %wk_hbm.1, bf16[44,176]{1,0:T(8,128)(2,1)} %wv_hbm.1, ...), custom_call_target="tpu_custom_call" | custom-call | flops 8000000000 | bytes 20000000 | tf_op jit(solution)/shard_map/pallas_call | solution.py:769
  147.0 0.0 copy-start
  147.0 1.7 %copy.22 = bf16[1,128,1408]{2,1,0:T(8,128)(2,1)} copy(bf16[1,128,1408]{2,1,0:T(8,128)(2,1)} %bitcast.7) | data formatting | bytes 720896
  148.8 0.0 copy-done
  148.8 0.6 copy.23
Async XLA Ops:
  147.0 1.8 %copy-start = (bf16[1,176]{1,0:T(2,128)(2,1)S(1)}, bf16[1,176]{1,0:T(2,128)(2,1)}, u32[]{:S(2)}) copy-start(bf16[1,176]{1,0:T(2,128)(2,1)} %get-tuple-element.9) | copy-start | bytes 1060

commit v2 on v1

--- a/solution.py
+++ b/solution.py
@@ -82,7 +82,7 @@
     tq_hbm, tk_hbm, tv_hbm, to_hbm, ck_hbm, cv_hbm, pos_hbm, table_hbm, turn_hbm,
     out, frame_out,
     patches, offset_in, piece_in, wq, wk, wv, wo, wu, wd, tq_w, tk_w, tv_w, to_w, ck_in, cv_in, pos_in, table, turn,
-    meta, xin, meta_in, src, src_in, pad, res, WA, WU, WU2, WD, WD2, C, comp, around, H1, KV, Q,
+    meta, xin, meta_in, src, src_in, pad, res, WA, WA2, WU, WU2, WD, WD2, C, comp, around, H1, KV, Q,
     SB, RB, RC, mixed, H2, HID, SB2, RB2, RC2,
     result, swapped, sums, pooled, qkv_send, qkv_recv, new_send, new_all, last_send, last_recv,
     local, big_send, big_recv, swap_send, swap_recv, s1, r1, s2, r2, s3, r3, s4, r4,
@@ -164,7 +164,9 @@
         ).astype(BF)
         term = dot(dot(grow, w[...]).astype(BF), to)
         total = term if total is None else total + term
-    WA[0, 0, place(0)] = total.astype(BF)
+    total = total.astype(BF)
+    WA[0, 0, place(0)] = total[:, 0:512]
+    WA2[0, place(0), 0] = total[:, 512:768]
 
     def z_first(B):
         def at(r):
@@ -279,7 +281,8 @@
             if tasks:
                 yield
 
-    load1, load4 = z_first(WA), x_first(C)
+    load4 = x_first(C)
+    load1 = both(z_first(WA), x_first(WA2))
     load2 = both(z_first(WU), x_first(WU2))
     load3 = both(z_first(WD), x_first(WD2))
     ahead(load1, 1)
@@ -376,16 +379,16 @@
 
     def gather(H):
         a, b = pl.ds(0, 64), pl.ds(64, 64)
-        one = copies.start(H.at[0, a], H.at[3, a], yp)
+        one = copies.start(H.at[0, a], H.at[2, a], yp)
         two = copies.start(H.at[0, b], H.at[1, b], ym)
         rest = [
-            copies.start(H.at[0, b], H.at[3, b], yp), copies.start(H.at[0, a], H.at[1, a], ym)
+            copies.start(H.at[0, b], H.at[2, b], yp), copies.start(H.at[0, a], H.at[1, a], ym)
         ]
         yield
         one.wait_recv()
-        far = [copies.start(H.at[3, a], H.at[2, a], yp)]
+        far = [copies.start(H.at[2, a], H.at[3, a], yp)]
         two.wait_recv()
-        far.append(copies.start(H.at[1, b], H.at[2, b], ym))
+        far.append(copies.start(H.at[1, b], H.at[3, b], ym))
         yield
         for copy in rest:
             copy.wait_recv()
@@ -400,11 +403,8 @@
     ahead(load1, 1)
     ahead(load2, 1)
     ahead(rows1, 1)
-    ahead(load2, 1)
-    drain(rows1)
     ahead(load1, 1)
     drain(load1)
-    ahead(load2, 1)
 
     plane_of = [c, 1 - c]
     x_of = [mod(k - x, 4) for k in range(4)]
@@ -430,13 +430,26 @@
         (r == 528 + lax.div(k, 128) * HD + at) & (at < HD), 1.0, 0.0
     ).astype(BF)
 
+    sides = []
+
+    def key_value(start, count):
+        rows = H1[start : start + count].reshape(count * TOK, DP)
+        spot = slice(start * TOK, (start + count) * TOK)
+        for at in range(2):
+            joined = jnp.concatenate(
+                [dot(rows, weight(WA, at, 128, 384)), dot(rows, weight(WA2, at, 0, 128))], axis=1
+            )
+            KV[0, at, spot, :] = dot(joined.astype(BF), wide_kv).astype(BF)
+            part = pl.ds(start * TOK, count * TOK)
+            sides.append(copies.start(KV.at[0, at, part], KV.at[1, at, part], sibling))
+
+    key_value(0, 3)
+    ahead(load2, 1)
+    drain(rows1)
+    key_value(3, 1)
+    ahead(load2, 1)
+    ahead(load3, 1)
     rows = H1[...].reshape(4 * TOK, DP)
-    sides = []
-    for at in range(2):
-        joined = dot(rows, weight(WA, at, 128, 512)).astype(BF)
-        KV[0, at] = dot(joined, wide_kv).astype(BF)
-        sides.append(copies.start(KV.at[0, at], KV.at[1, at], sibling))
-    ahead(load3, 1)
     for at in range(2):
         joined = dot(rows, weight(WA, at, 0, 256)).astype(BF)
         Q[at] = dot(joined, wide_q).astype(BF).reshape(4, TOK, 256)
@@ -444,14 +457,14 @@
     for copy in sides:
         copy.wait_recv()
 
-    def attend(block):
+    def attend(block, count=1):
         total = None
         for at in range(2):
             heads = []
             for h in range(2):
                 span = slice(h * 128, h * 128 + 128)
                 vspan = slice(256 + h * 128, 256 + h * 128 + 128)
-                q = Q[at, block, :, span]
+                q = Q[at, block : block + count, :, span].reshape(count * TOK, 128)
                 s = [dot_nt(q, KV[k, at, :, span]) for k in range(2)]
                 top = jnp.maximum(
                     jnp.max(s[0], axis=1, keepdims=True), jnp.max(s[1], axis=1, keepdims=True)
@@ -463,7 +476,7 @@
                 )
                 heads.append((o / mass).astype(BF))
             both_heads = dot(jnp.concatenate(heads, axis=1), narrow).astype(BF)
-            term = dot_nt(both_heads, weight(WA, at, 512, 256))
+            term = dot_nt(both_heads, weight(WA2, at, 0, 256))
             total = term if total is None else total + term
         return total
 
@@ -471,16 +484,17 @@
         a, b = pl.ds(0, 64), pl.ds(64, 64)
 
         def send_far():
-            S[0] = partial(2).astype(BF)
+            S[0] = partial(3, 1).astype(BF)
             return [
                 copies.start(S.at[0, a], B.at[0], yp), copies.start(S.at[0, b], B.at[1], ym)
             ]
 
         def send_near():
-            S[1] = partial(1).astype(BF)
-            one = copies.start(S.at[1, b], R.at[0, b], yp)
-            S[2] = partial(3).astype(BF)
-            return [one, copies.start(S.at[2, a], R.at[1, a], ym)]
+            pair = partial(1, 2).astype(BF)
+            S[1], S[2] = pair[0:TOK], pair[TOK:]
+            return [
+                copies.start(S.at[1, b], R.at[0, b], yp), copies.start(S.at[2, a], R.at[1, a], ym)
+            ]
 
         if far_first:
             far = send_far()
@@ -497,7 +511,7 @@
         far[1].wait_recv()
         S[2, 64:128, :] = (S[2, 64:128, :].astype(F32) + B[1].astype(F32)).astype(BF)
         near.append(copies.start(S.at[2, b], R.at[1, b], ym))
-        own = partial(0)
+        own = partial(0, 1)
         between(2)
         for copy in near:
             copy.wait_recv()
@@ -524,8 +538,8 @@
     ahead(load3, 1)
     ahead(load4, 1)
 
-    def up(block, at):
-        rows = H2[block]
+    def up(block, count, at):
+        rows = H2[block : block + count].reshape(count * TOK, DP)
         return [
             jax.nn.gelu(dot(rows, weight(WU, at, 0, 512))).astype(BF),
             jax.nn.gelu(dot(rows, weight(WU2, at, 0, 256))).astype(BF),
@@ -536,11 +550,11 @@
             hidden[1], weight(WD2, at, 0, 256)
         )
 
-    def up_down(block):
-        return down(up(block, 0), 0) + down(up(block, 1), 1)
+    def up_down(block, count):
+        return down(up(block, count, 0), 0) + down(up(block, count, 1), 1)
 
     for at in range(2):
-        first, second = up(0, at)
+        first, second = up(0, 1, at)
         HID[at, :, 0:512] = first
         HID[at, :, 512:768] = second
     ahead(rows2, 1)
@@ -550,17 +564,17 @@
     ahead(load3, 1)
     drain(load3)
 
-    def near_rows(block):
-        return up_down(block)
-
-    def far_rows(block):
+    def far_rows():
         ahead(load4, 1)
         drain(rows2)
-        return up_down(block)
-
-    def own_rows(block):
+        return up_down(3, 1)
+
+    def own_rows():
         own = [(HID[at, :, 0:512], HID[at, :, 512:768]) for at in range(2)]
         return down(own[0], 0) + down(own[1], 1)
+
+    def mlp(block, count):
+        return own_rows() if block == 0 else up_down(1, 2) if block == 1 else far_rows()
 
     def beside_mlp(n):
         if n == 0:
@@ -569,8 +583,7 @@
             ahead(load4, 1)
             copies.retire(8)
 
-    calls = [near_rows, near_rows, far_rows, own_rows]
-    total = scatter(lambda block: calls.pop(0)(block), SB2, RB2, RC2, False, beside_mlp)
+    total = scatter(mlp, SB2, RB2, RC2, False, beside_mlp)
     last = (mixed[...].astype(F32) + total).astype(BF)
     columns = [
         dot_nt(last[:, q * QW : (q + 1) * QW], pad[q, 0:size, :])
@@ -756,7 +769,7 @@
         kept.wait()
 
 
-BIG = 160
+BIG = 176
 
 
 def call(*operands):
@@ -783,7 +796,8 @@
             pltpu.VMEM((TOK, QW), BF),
             pltpu.VMEM((4, 512, QW), BF),
             pltpu.VMEM((TOK, DP), BF),
-            pltpu.VMEM((2, 4, 8, W_ROWS, WC), BF),
+            pltpu.VMEM((2, 4, 8, W_ROWS, 512), BF),
+            pltpu.VMEM((2, 8, 4, W_ROWS, 256), BF),
             pltpu.VMEM((2, 4, 8, W_ROWS, 512), BF),
             pltpu.VMEM((2, 8, 4, W_ROWS, 256), BF),
             pltpu.VMEM((2, 4, 8, W_ROWS, 512), BF),

time: 149 us -> 154 us (1.034)
  Pallas kernels: 146 us -> 151 us
    pallas_call x1, Pallas kernels: 146 us -> 151 us  [call(): pl.pallas_call(kernel, out_shape=(jax.ShapeDtypeStruct((TOK, D), BF), jax...]
where the time goes in v2:
time: 154 us
  Pallas kernels  151 us (98%)
  local copies, waits for them, and re-layouts  2.31 us (2%)
    pallas_call x1, Pallas kernels, call(): pl.pallas_call(kernel, out_shape=(jax.ShapeDtypeStruct((TOK, D), BF), jax...  151 us

profile of v2, /device:TPU:1, one launch (start us, length us, event | category | flops | bytes accessed | tf_op | source)
XLA Modules:
  0.0 153.8 jit_solution(17639122866674851788)
XLA Ops:
  0.6 150.8 %shard_map.185 = (bf16[128,1408]{1,0:T(8,128)(2,1)}, bf16[1,176]{1,0:T(2,128)(2,1)}) custom-call(bf16[128,1408]{1,0:T(8,128)(2,1)} %bitcast.8, s32[1,128]{1,0:T(1,128)} %bitcast.11, s32[1,128]{1,0:T(1,128)} %bitcast.12, bf16[44,176]{1,0:T(8,128)(2,1)} %wq_hbm.1, bf16[44,176]{1,0:T(8,128)(2,1)} %wk_hbm.1, bf16[44,176]{1,0:T(8,128)(2,1)} %wv_hbm.1, ...), custom_call_target="tpu_custom_call" | custom-call | flops 8000000000 | bytes 20000000 | tf_op jit(solution)/shard_map/pallas_call | solution.py:782
  151.5 0.0 copy-start
  151.5 1.7 %copy.22 = bf16[1,128,1408]{2,1,0:T(8,128)(2,1)} copy(bf16[1,128,1408]{2,1,0:T(8,128)(2,1)} %bitcast.7) | data formatting | bytes 720896
  153.2 0.0 copy-done
  153.2 0.6 copy.23
Async XLA Ops:
  151.5 1.8 %copy-start = (bf16[1,176]{1,0:T(2,128)(2,1)S(1)}, bf16[1,176]{1,0:T(2,128)(2,1)}, u32[]{:S(2)}) copy-start(bf16[1,176]{1,0:T(2,128)(2,1)} %get-tuple-element.9) | copy-start | bytes 1060

commit v3 on v2

--- a/solution.py
+++ b/solution.py
@@ -41,6 +41,27 @@
     return lax.rem(a + n, n)
 
 
+def remote(src, dst, send, recv, device):
+    return pltpu.make_async_remote_copy(
+        src_ref=src, dst_ref=dst, send_sem=send, recv_sem=recv,
+        device_id=device, device_id_type=MESH,
+    )
+
+
+class Leg:
+    def __init__(self, src, dst, device, send, recv):
+        self.ends = (src, dst, send, recv, device)
+
+    def start(self):
+        remote(*self.ends).start()
+
+    def wait_recv(self):
+        remote(*self.ends).wait_recv()
+
+    def wait_send(self):
+        remote(*self.ends).wait_send()
+
+
 class Copies:
     def __init__(self, send, recv):
         self.send, self.recv, self.used, self.open = send, recv, 0, []
@@ -82,10 +103,10 @@
     tq_hbm, tk_hbm, tv_hbm, to_hbm, ck_hbm, cv_hbm, pos_hbm, table_hbm, turn_hbm,
     out, frame_out,
     patches, offset_in, piece_in, wq, wk, wv, wo, wu, wd, tq_w, tk_w, tv_w, to_w, ck_in, cv_in, pos_in, table, turn,
-    meta, xin, meta_in, src, src_in, pad, res, WA, WA2, WU, WU2, WD, WD2, C, comp, around, H1, KV, Q,
+    meta, xin, meta_in, src, src_in, via_patches, via_src, pad, res, WA, WU, WU2, WD, WD2, C, comp, around, H1, KV, Q,
     SB, RB, RC, mixed, H2, HID, SB2, RB2, RC2,
     result, swapped, sums, pooled, qkv_send, qkv_recv, new_send, new_all, last_send, last_recv,
-    local, big_send, big_recv, swap_send, swap_recv, s1, r1, s2, r2, s3, r3, s4, r4,
+    local, big_send, big_recv, swap_send, swap_recv, leg_send, leg_recv, s1, r1, s2, r2, s3, r3, s4, r4,
 ):
     f = lax.axis_index("frame")
     t = lax.axis_index("tok")
@@ -119,10 +140,11 @@
     zp, zm = dev(x, mod(z + 1, 8), y, c), dev(x, mod(z - 1, 8), y, c)
     sibling = dev(x, z, y, 1 - c)
     partner = dev(x, mod(z + 4, 8), y, 1 - c)
+    target_up, target_down = dev(x, mod(z + 3, 8), y, 1 - c), dev(x, mod(z - 3, 8), y, 1 - c)
     after, before = (mod(f + 1, 32), t), (mod(f - 1, 32), t)
 
     barrier = pltpu.get_barrier_semaphore()
-    friends = (xp, xm, yp, ym, zp, zm, sibling, partner, after, before)
+    friends = (xp, xm, yp, ym, zp, zm, sibling, partner, target_up, target_down, after, before)
     for friend in friends:
         pl.semaphore_signal(barrier, inc=1, device_id=friend, device_id_type=MESH)
     pl.semaphore_wait(barrier, len(friends))
@@ -130,14 +152,36 @@
     copies = Copies(big_send, big_recv)
     moves = c != zh
 
-    def remote(src, dst, send, recv, device):
-        return pltpu.make_async_remote_copy(
-            src_ref=src, dst_ref=dst, send_sem=send, recv_sem=recv,
-            device_id=device, device_id_type=MESH,
-        )
-
     def swap(src, dst, n):
         return remote(src, dst, swap_send.at[n], swap_recv.at[n], partner)
+
+    carries_up = c != lax.div(mod(z - 1, 8), 4)
+    carries_down = c != lax.div(mod(z + 1, 8), 4)
+    first_rows, last_rows = pl.ds(0, 64), pl.ds(64, 64)
+
+    def legs(n, a, via, b):
+        sends = (
+            (a.at[first_rows], via.at[0], zp), (a.at[last_rows], via.at[1], zm),
+            (via.at[0], b.at[first_rows], target_up), (via.at[1], b.at[last_rows], target_down),
+        )
+        return [Leg(*ends, leg_send.at[n + k], leg_recv.at[n + k]) for k, ends in enumerate(sends)]
+
+    def hand_on(make):
+        @pl.when(carries_up)
+        def _():
+            make()[0].wait_recv()
+            make()[2].start()
+
+        @pl.when(carries_down)
+        def _():
+            make()[1].wait_recv()
+            make()[3].start()
+
+    def patch_legs():
+        return legs(0, patches, via_patches, xin)
+
+    def src_legs():
+        return legs(4, src, via_src, src_in)
 
     for load in loads[0:3]:
         load.wait()
@@ -146,7 +190,8 @@
 
     @pl.when(moves)
     def _():
-        swap(patches, xin, 0).start()
+        for leg in patch_legs()[0:2]:
+            leg.start()
         swap(meta, meta_in, 1).start()
 
     @pl.when(jnp.logical_not(moves))
@@ -164,9 +209,7 @@
         ).astype(BF)
         term = dot(dot(grow, w[...]).astype(BF), to)
         total = term if total is None else total + term
-    total = total.astype(BF)
-    WA[0, 0, place(0)] = total[:, 0:512]
-    WA2[0, place(0), 0] = total[:, 512:768]
+    WA[0, 0, place(0)] = total.astype(BF)
 
     def z_first(B):
         def at(r):
@@ -281,11 +324,11 @@
             if tasks:
                 yield
 
-    load4 = x_first(C)
-    load1 = both(z_first(WA), x_first(WA2))
+    load1, load4 = z_first(WA), x_first(C)
     load2 = both(z_first(WU), x_first(WU2))
     load3 = both(z_first(WD), x_first(WD2))
     ahead(load1, 1)
+    hand_on(patch_legs)
 
     for q, (start, size) in enumerate(WINDOWS):
         r, k = iota((size, QW), 0) + start, iota((size, QW), 1)
@@ -330,13 +373,15 @@
 
     @pl.when(moves)
     def _():
-        swap(src, src_in, 2).start()
+        for leg in src_legs()[0:2]:
+            leg.start()
 
     @pl.when(jnp.logical_not(moves))
     def _():
         src_in[...] = src[...]
 
     ahead(load1, 1)
+    hand_on(src_legs)
 
     def turned(v):
         return jnp.concatenate([v[:, 44:88], v[:, 0:44], v[:, 132:176], v[:, 88:132]], axis=1)
@@ -366,9 +411,9 @@
 
     @pl.when(moves)
     def _():
-        swap(patches, xin, 0).wait()
         swap(meta, meta_in, 1).wait()
-        swap(src, src_in, 2).wait()
+        for leg in patch_legs()[2:4] + src_legs()[2:4]:
+            leg.wait_recv()
 
     quarters = padded(xin)
     piece = as_column(meta_in[1:2, :])
@@ -436,10 +481,8 @@
         rows = H1[start : start + count].reshape(count * TOK, DP)
         spot = slice(start * TOK, (start + count) * TOK)
         for at in range(2):
-            joined = jnp.concatenate(
-                [dot(rows, weight(WA, at, 128, 384)), dot(rows, weight(WA2, at, 0, 128))], axis=1
-            )
-            KV[0, at, spot, :] = dot(joined.astype(BF), wide_kv).astype(BF)
+            joined = dot(rows, weight(WA, at, 128, 512)).astype(BF)
+            KV[0, at, spot, :] = dot(joined, wide_kv).astype(BF)
             part = pl.ds(start * TOK, count * TOK)
             sides.append(copies.start(KV.at[0, at, part], KV.at[1, at, part], sibling))
 
@@ -476,7 +519,7 @@
                 )
                 heads.append((o / mass).astype(BF))
             both_heads = dot(jnp.concatenate(heads, axis=1), narrow).astype(BF)
-            term = dot_nt(both_heads, weight(WA2, at, 0, 256))
+            term = dot_nt(both_heads, weight(WA, at, 512, 256))
             total = term if total is None else total + term
         return total
 
@@ -742,6 +785,21 @@
         kept.start()
 
     copies.retire()
+
+    @pl.when(moves)
+    def _():
+        for leg in patch_legs()[0:2] + src_legs()[0:2]:
+            leg.wait_send()
+
+    @pl.when(carries_up)
+    def _():
+        patch_legs()[2].wait_send()
+        src_legs()[2].wait_send()
+
+    @pl.when(carries_down)
+    def _():
+        patch_legs()[3].wait_send()
+        src_legs()[3].wait_send()
 
     @pl.when(moves)
     def _():
@@ -794,10 +852,11 @@
             pltpu.VMEM((2, TOK), F32),
             pltpu.VMEM((TOK, QW), BF),
             pltpu.VMEM((TOK, QW), BF),
+            pltpu.VMEM((2, 64, D), BF),
+            pltpu.VMEM((2, 64, QW), BF),
             pltpu.VMEM((4, 512, QW), BF),
             pltpu.VMEM((TOK, DP), BF),
-            pltpu.VMEM((2, 4, 8, W_ROWS, 512), BF),
-            pltpu.VMEM((2, 8, 4, W_ROWS, 256), BF),
+            pltpu.VMEM((2, 4, 8, W_ROWS, WC), BF),
             pltpu.VMEM((2, 4, 8, W_ROWS, 512), BF),
             pltpu.VMEM((2, 8, 4, W_ROWS, 256), BF),
             pltpu.VMEM((2, 4, 8, W_ROWS, 512), BF),
@@ -830,6 +889,7 @@
             dma((len(operands),)),
             dma((BIG,)), dma((BIG,)),
             dma((4,)), dma((4,)),
+            dma((8,)), dma((8,)),
             dma, dma, dma, dma, dma, dma, dma, dma,
         ],
         compiler_params=pltpu.CompilerParams(

time: 154 us -> 154 us (level)
  no operation moved by 1% of the time
where the time goes in v3:
time: 154 us
  Pallas kernels  151 us (98%)
  local copies, waits for them, and re-layouts  2.31 us (2%)
    pallas_call x1, Pallas kernels, call(): pl.pallas_call(kernel, out_shape=(jax.ShapeDtypeStruct((TOK, D), BF), jax...  151 us

profile of v3, /device:TPU:1, one launch (start us, length us, event | category | flops | bytes accessed | tf_op | source)
XLA Modules:
  0.0 154.0 jit_solution(3699867448233593931)
XLA Ops:
  0.6 151.0 %shard_map.185 = (bf16[128,1408]{1,0:T(8,128)(2,1)}, bf16[1,176]{1,0:T(2,128)(2,1)}) custom-call(bf16[128,1408]{1,0:T(8,128)(2,1)} %bitcast.8, s32[1,128]{1,0:T(1,128)} %bitcast.11, s32[1,128]{1,0:T(1,128)} %bitcast.12, bf16[44,176]{1,0:T(8,128)(2,1)} %wq_hbm.1, bf16[44,176]{1,0:T(8,128)(2,1)} %wk_hbm.1, bf16[44,176]{1,0:T(8,128)(2,1)} %wv_hbm.1, ...), custom_call_target="tpu_custom_call" | custom-call | flops 8000000000 | bytes 20000000 | tf_op jit(solution)/shard_map/pallas_call | solution.py:840
  151.6 0.0 copy-start
  151.7 1.7 %copy.22 = bf16[1,128,1408]{2,1,0:T(8,128)(2,1)} copy(bf16[1,128,1408]{2,1,0:T(8,128)(2,1)} %bitcast.7) | data formatting | bytes 720896
  153.4 0.0 copy-done
  153.4 0.6 copy.23
Async XLA Ops:
  151.6 1.8 %copy-start = (bf16[1,176]{1,0:T(2,128)(2,1)S(1)}, bf16[1,176]{1,0:T(2,128)(2,1)}, u32[]{:S(2)}) copy-start(bf16[1,176]{1,0:T(2,128)(2,1)} %get-tuple-element.9) | copy-start | bytes 1060

commit v4 on v3

--- a/solution.py
+++ b/solution.py
@@ -66,19 +66,16 @@
     def __init__(self, send, recv):
         self.send, self.recv, self.used, self.open = send, recv, 0, []
 
-    def start(self, src, dst, device):
+    def make(self, src, dst, device):
         n = self.used
         self.used += 1
-        copy = pltpu.make_async_remote_copy(
-            src_ref=src,
-            dst_ref=dst,
-            send_sem=self.send.at[n],
-            recv_sem=self.recv.at[n],
-            device_id=device,
-            device_id_type=MESH,
-        )
+        copy = Leg(src, dst, device, self.send.at[n], self.recv.at[n])
+        self.open.append(copy)
+        return copy
+
+    def start(self, src, dst, device):
+        copy = self.make(src, dst, device)
         copy.start()
-        self.open.append(copy)
         return copy
 
     def retire(self, keep=0):
@@ -103,8 +100,8 @@
     tq_hbm, tk_hbm, tv_hbm, to_hbm, ck_hbm, cv_hbm, pos_hbm, table_hbm, turn_hbm,
     out, frame_out,
     patches, offset_in, piece_in, wq, wk, wv, wo, wu, wd, tq_w, tk_w, tv_w, to_w, ck_in, cv_in, pos_in, table, turn,
-    meta, xin, meta_in, src, src_in, via_patches, via_src, pad, res, WA, WU, WU2, WD, WD2, C, comp, around, H1, KV, Q,
-    SB, RB, RC, mixed, H2, HID, SB2, RB2, RC2,
+    meta, xin, meta_in, src, src_in, via_patches, via_src, pad, res, WA, WA2, WU, WU2, WD, WD2, C, comp, around, H1, KV, Q,
+    SB, RB, RC, mixed, H2, HID, PB, SB2, RB2, RC2,
     result, swapped, sums, pooled, qkv_send, qkv_recv, new_send, new_all, last_send, last_recv,
     local, big_send, big_recv, swap_send, swap_recv, leg_send, leg_recv, s1, r1, s2, r2, s3, r3, s4, r4,
 ):
@@ -194,11 +191,6 @@
             leg.start()
         swap(meta, meta_in, 1).start()
 
-    @pl.when(jnp.logical_not(moves))
-    def _():
-        xin[...] = patches[...]
-        meta_in[...] = meta[...]
-
     for load in loads[3:7]:
         load.wait()
     grow = jnp.where(iota((48, 44), 0) == iota((48, 44), 1), 1.0, 0.0).astype(BF)
@@ -209,7 +201,9 @@
         ).astype(BF)
         term = dot(dot(grow, w[...]).astype(BF), to)
         total = term if total is None else total + term
-    WA[0, 0, place(0)] = total.astype(BF)
+    total = total.astype(BF)
+    WA[0, 0, place(0)] = total[:, 0:640]
+    WA2[0, place(0), 0] = total[:, 640:768]
 
     def z_first(B):
         def at(r):
@@ -223,8 +217,8 @@
             firsts.append(copies.start(B.at[0, 0, run], B.at[0, 3, run], xp))
             firsts.append(copies.start(B.at[0, 0, run], B.at[0, 1, run], xm))
 
-        half = B.shape[4] // 2
-        low, high = pl.ds(0, half), pl.ds(half, half)
+        half = B.shape[4] // 256 * 128
+        low, high = pl.ds(0, half), pl.ds(half, B.shape[4] - half)
         for step in range(1, 5):
             for copy in waits:
                 copy.wait_recv()
@@ -273,13 +267,12 @@
             copies.start(B.at[0, here, 0], B.at[0, here, 1], xm),
         ]
         yield
-        half = B.shape[4] // 2
-        low, high = pl.ds(0, half), pl.ds(half, half)
+        low, high = pl.ds(0, 32), pl.ds(32, B.shape[3] - 32)
         for copy in waits:
             copy.wait_recv()
         waits = [
-            copies.start(B.at[0, here, 3, :, low], B.at[0, here, 2, :, low], xp),
-            copies.start(B.at[0, here, 1, :, high], B.at[0, here, 2, :, high], xm),
+            copies.start(B.at[0, here, 3, low], B.at[0, here, 2, low], xp),
+            copies.start(B.at[0, here, 1, high], B.at[0, here, 2, high], xm),
         ]
         yield
 
@@ -324,10 +317,11 @@
             if tasks:
                 yield
 
-    load1, load4 = z_first(WA), x_first(C)
+    load1, load_out, load4 = z_first(WA), x_first(WA2), x_first(C)
     load2 = both(z_first(WU), x_first(WU2))
     load3 = both(z_first(WD), x_first(WD2))
     ahead(load1, 1)
+    ahead(load_out, 1)
     hand_on(patch_legs)
 
     for q, (start, size) in enumerate(WINDOWS):
@@ -351,6 +345,8 @@
     for q in range(1, 4):
         mine = jnp.where(piece == float(q), quarters[q], mine)
     comp[...] = mine.astype(BF)
+    for q in range(4):
+        H1[0, :, q * QW : (q + 1) * QW] = quarters[q].astype(BF)
     hops = [
         copies.start(comp, around.at[0], after),
         copies.start(comp, around.at[1], before),
@@ -362,6 +358,7 @@
         one[0, 0, place(0)] = rows[:, 0:512]
         two[0, place(0), 0] = rows[:, 512:768]
     ahead(load1, 1)
+    ahead(load_out, 1)
     for copy in hops:
         copy.wait_recv()
     earlier = jnp.where(f > 0, around[0].astype(F32), 0.0)
@@ -371,14 +368,53 @@
     )
     src[...] = source.astype(BF)
 
+    def gather(H):
+        a, b = pl.ds(0, 64), pl.ds(64, 64)
+        one = copies.make(H.at[0, a], H.at[2, a], yp)
+        two = copies.make(H.at[0, b], H.at[1, b], ym)
+        rest = [
+            copies.make(H.at[0, b], H.at[2, b], yp), copies.make(H.at[0, a], H.at[1, a], ym)
+        ]
+        far = [
+            copies.make(H.at[2, a], H.at[3, a], yp), copies.make(H.at[1, b], H.at[3, b], ym)
+        ]
+
+        def begin():
+            for copy in (one, two, *rest):
+                copy.start()
+
+        def forward():
+            one.wait_recv()
+            far[0].start()
+            two.wait_recv()
+            far[1].start()
+
+        def near():
+            for copy in rest:
+                copy.wait_recv()
+
+        def last():
+            for copy in far:
+                copy.wait_recv()
+
+        return begin, forward, near, last
+
+    begin1, forward1, near1, last1 = gather(H1)
+    stays = jnp.logical_not(moves)
+
     @pl.when(moves)
     def _():
         for leg in src_legs()[0:2]:
             leg.start()
 
-    @pl.when(jnp.logical_not(moves))
-    def _():
-        src_in[...] = src[...]
+    @pl.when(stays)
+    def _():
+        for q in range(4):
+            columns = slice(q * QW, (q + 1) * QW)
+            H1[0, :, columns] = jnp.where(
+                piece == float(q), src[...].astype(F32), H1[0, :, columns].astype(F32)
+            ).astype(BF)
+        begin1()
 
     ahead(load1, 1)
     hand_on(src_legs)
@@ -409,47 +445,34 @@
     C[0, place(0), 0, 0:62, 256:432] = cv_in[...]
     ahead(load1, 2)
 
+    pl.when(stays)(forward1)
+
     @pl.when(moves)
     def _():
         swap(meta, meta_in, 1).wait()
         for leg in patch_legs()[2:4] + src_legs()[2:4]:
             leg.wait_recv()
-
-    quarters = padded(xin)
-    piece = as_column(meta_in[1:2, :])
-    for q in range(4):
-        H1[0, :, q * QW : (q + 1) * QW] = jnp.where(
-            piece == float(q), src_in[...].astype(F32), quarters[q]
-        ).astype(BF)
-
-    def gather(H):
-        a, b = pl.ds(0, 64), pl.ds(64, 64)
-        one = copies.start(H.at[0, a], H.at[2, a], yp)
-        two = copies.start(H.at[0, b], H.at[1, b], ym)
-        rest = [
-            copies.start(H.at[0, b], H.at[2, b], yp), copies.start(H.at[0, a], H.at[1, a], ym)
-        ]
-        yield
-        one.wait_recv()
-        far = [copies.start(H.at[2, a], H.at[3, a], yp)]
-        two.wait_recv()
-        far.append(copies.start(H.at[1, b], H.at[3, b], ym))
-        yield
-        for copy in rest:
-            copy.wait_recv()
-        yield
-        for copy in far:
-            copy.wait_recv()
-
-    rows1 = gather(H1)
-    ahead(rows1, 1)
+        quarters = padded(xin)
+        piece = as_column(meta_in[1:2, :])
+        for q in range(4):
+            H1[0, :, q * QW : (q + 1) * QW] = jnp.where(
+                piece == float(q), src_in[...].astype(F32), quarters[q]
+            ).astype(BF)
+        begin1()
+
+    ahead(load_out, 1)
     ahead(load2, 2)
-    ahead(rows1, 1)
+    pl.when(moves)(forward1)
     ahead(load1, 1)
     ahead(load2, 1)
-    ahead(rows1, 1)
+    ahead(load_out, 1)
+    near1()
+    ahead(load2, 1)
+    ahead(load_out, 1)
+    last1()
     ahead(load1, 1)
     drain(load1)
+    ahead(load2, 1)
 
     plane_of = [c, 1 - c]
     x_of = [mod(k - x, 4) for k in range(4)]
@@ -486,19 +509,20 @@
             part = pl.ds(start * TOK, count * TOK)
             sides.append(copies.start(KV.at[0, at, part], KV.at[1, at, part], sibling))
 
-    key_value(0, 3)
-    ahead(load2, 1)
-    drain(rows1)
-    key_value(3, 1)
-    ahead(load2, 1)
+    key_value(0, 4)
+    ahead(load_out, 1)
     ahead(load3, 1)
     rows = H1[...].reshape(4 * TOK, DP)
     for at in range(2):
         joined = dot(rows, weight(WA, at, 0, 256)).astype(BF)
         Q[at] = dot(joined, wide_q).astype(BF).reshape(4, TOK, 256)
+    ahead(load_out, 1)
     ahead(load3, 1)
     for copy in sides:
         copy.wait_recv()
+    drain(load_out)
+    ahead(load2, 1)
+    ahead(load3, 1)
 
     def attend(block, count=1):
         total = None
@@ -519,7 +543,9 @@
                 )
                 heads.append((o / mass).astype(BF))
             both_heads = dot(jnp.concatenate(heads, axis=1), narrow).astype(BF)
-            term = dot_nt(both_heads, weight(WA, at, 512, 256))
+            term = dot_nt(both_heads[:, 0:128], weight(WA, at, 512, 128)) + dot_nt(
+                both_heads[:, 128:256], weight(WA2, at, 0, 128)
+            )
             total = term if total is None else total + term
         return total
 
@@ -533,17 +559,22 @@
             ]
 
         def send_near():
-            pair = partial(1, 2).astype(BF)
-            S[1], S[2] = pair[0:TOK], pair[TOK:]
-            return [
-                copies.start(S.at[1, b], R.at[0, b], yp), copies.start(S.at[2, a], R.at[1, a], ym)
-            ]
+            if far_first:
+                S[1] = partial(1, 1).astype(BF)
+                one = copies.start(S.at[1, b], R.at[0, b], yp)
+                between(1)
+                S[2] = partial(2, 1).astype(BF)
+            else:
+                pair = partial(1, 2).astype(BF)
+                S[1], S[2] = pair[0:TOK], pair[TOK:]
+                one = copies.start(S.at[1, b], R.at[0, b], yp)
+            return [one, copies.start(S.at[2, a], R.at[1, a], ym)]
 
         if far_first:
             far = send_far()
             between(0)
             near = send_near()
-            between(1)
+            between(2)
         else:
             near = send_near()
             far = send_far()
@@ -555,29 +586,29 @@
         S[2, 64:128, :] = (S[2, 64:128, :].astype(F32) + B[1].astype(F32)).astype(BF)
         near.append(copies.start(S.at[2, b], R.at[1, b], ym))
         own = partial(0, 1)
-        between(2)
+        between(3)
         for copy in near:
             copy.wait_recv()
         return own + R[0].astype(F32) + R[1].astype(F32)
 
     def beside_attention(n):
         if n == 0:
+            ahead(load3, 1)
+        elif n == 1:
             ahead(load2, 1)
             ahead(load3, 1)
-            ahead(load4, 1)
-        elif n == 1:
-            ahead(load3, 1)
-            ahead(load2, 1)
+        elif n == 2:
+            drain(load2)
             ahead(load4, 1)
         else:
             ahead(load3, 1)
-            drain(load2)
+            ahead(load4, 1)
 
     total = scatter(attend, SB, RB, RC, True, beside_attention)
     mixed[...] = (res[...].astype(F32) + total).astype(BF)
     H2[0] = norm_padded(mixed[...].astype(F32), valid).astype(BF)
-    rows2 = gather(H2)
-    ahead(rows2, 1)
+    begin2, forward2, near2, last2 = gather(H2)
+    begin2()
     ahead(load3, 1)
     ahead(load4, 1)
 
@@ -600,31 +631,26 @@
         first, second = up(0, 1, at)
         HID[at, :, 0:512] = first
         HID[at, :, 512:768] = second
-    ahead(rows2, 1)
-    copies.retire(24)
-    ahead(load4, 1)
-    ahead(rows2, 1)
-    ahead(load3, 1)
+    forward2()
     drain(load3)
+    own = [(HID[at, :, 0:512], HID[at, :, 512:768]) for at in range(2)]
+    PB[...] = down(own[0], 0) + down(own[1], 1)
+    copies.retire(28)
+    near2()
 
     def far_rows():
         ahead(load4, 1)
-        drain(rows2)
+        last2()
         return up_down(3, 1)
 
-    def own_rows():
-        own = [(HID[at, :, 0:512], HID[at, :, 512:768]) for at in range(2)]
-        return down(own[0], 0) + down(own[1], 1)
-
     def mlp(block, count):
-        return own_rows() if block == 0 else up_down(1, 2) if block == 1 else far_rows()
+        return PB[...] if block == 0 else up_down(1, 2) if block == 1 else far_rows()
 
     def beside_mlp(n):
-        if n == 0:
+        ahead(load4, 1)
+        if n == 3:
+            copies.retire(12)
             ahead(load4, 1)
-        else:
-            ahead(load4, 1)
-            copies.retire(8)
 
     total = scatter(mlp, SB2, RB2, RC2, False, beside_mlp)
     last = (mixed[...].astype(F32) + total).astype(BF)
@@ -856,7 +882,8 @@
             pltpu.VMEM((2, 64, QW), BF),
             pltpu.VMEM((4, 512, QW), BF),
             pltpu.VMEM((TOK, DP), BF),
-            pltpu.VMEM((2, 4, 8, W_ROWS, WC), BF),
+            pltpu.VMEM((2, 4, 8, W_ROWS, 640), BF),
+            pltpu.VMEM((2, 8, 4, W_ROWS, 128), BF),
             pltpu.VMEM((2, 4, 8, W_ROWS, 512), BF),
             pltpu.VMEM((2, 8, 4, W_ROWS, 256), BF),
             pltpu.VMEM((2, 4, 8, W_ROWS, 512), BF),
@@ -873,6 +900,7 @@
             pltpu.VMEM((TOK, DP), BF),
             pltpu.VMEM((4, TOK, DP), BF),
             pltpu.VMEM((2, TOK, 768), BF),
+            pltpu.VMEM((TOK, DP), F32),
             pltpu.VMEM((3, TOK, DP), BF),
             pltpu.VMEM((2, 64, DP), BF),
             pltpu.VMEM((2, TOK, DP), BF),

time: 154 us -> 158 us (1.026)
  Pallas kernels: 151 us -> 155 us
    pallas_call x1, Pallas kernels: 151 us -> 155 us  [call(): pl.pallas_call(kernel, out_shape=(jax.ShapeDtypeStruct((TOK, D), BF), jax...]
where the time goes in v4:
time: 158 us; the launch traced here: 157 us
  Pallas kernels  155 us (98%)
  local copies, waits for them, and re-layouts  2.31 us (1%)
    pallas_call x1, Pallas kernels, call(): pl.pallas_call(kernel, out_shape=(jax.ShapeDtypeStruct((TOK, D), BF), jax...  155 us

profile of v4, /device:TPU:1, one launch (start us, length us, event | category | flops | bytes accessed | tf_op | source)
XLA Modules:
  0.0 157.5 jit_solution(13295819258151869229)
XLA Ops:
  0.6 154.5 %shard_map.185 = (bf16[128,1408]{1,0:T(8,128)(2,1)}, bf16[1,176]{1,0:T(2,128)(2,1)}) custom-call(bf16[128,1408]{1,0:T(8,128)(2,1)} %bitcast.8, s32[1,128]{1,0:T(1,128)} %bitcast.11, s32[1,128]{1,0:T(1,128)} %bitcast.12, bf16[44,176]{1,0:T(8,128)(2,1)} %wq_hbm.1, bf16[44,176]{1,0:T(8,128)(2,1)} %wk_hbm.1, bf16[44,176]{1,0:T(8,128)(2,1)} %wv_hbm.1, ...), custom_call_target="tpu_custom_call" | custom-call | flops 8000000000 | bytes 20000000 | tf_op jit(solution)/shard_map/pallas_call | solution.py:866
  155.2 0.0 copy-start
  155.2 1.7 %copy.22 = bf16[1,128,1408]{2,1,0:T(8,128)(2,1)} copy(bf16[1,128,1408]{2,1,0:T(8,128)(2,1)} %bitcast.7) | data formatting | bytes 720896
  156.9 0.0 copy-done
  156.9 0.6 copy.23
Async XLA Ops:
  155.2 1.8 %copy-start = (bf16[1,176]{1,0:T(2,128)(2,1)S(1)}, bf16[1,176]{1,0:T(2,128)(2,1)}, u32[]{:S(2)}) copy-start(bf16[1,176]{1,0:T(2,128)(2,1)} %get-tuple-element.9) | copy-start | bytes 1060

commit v5 on v1

--- a/solution.py
+++ b/solution.py
@@ -21,7 +21,7 @@
 F32 = jnp.float32
 BF = jnp.bfloat16
 WC = 768
-W_ROWS, CACHE_ROWS, CACHE_COLS = 48, 64, 512
+W_ROWS, CACHE_ROWS, CACHE_COLS = 48, 64, 384
 WINDOWS = ((0, 384), (256, 512), (640, 512), (1024, 384))
 
 
@@ -39,25 +39,43 @@
 
 def mod(a, n):
     return lax.rem(a + n, n)
+
+
+def remote(src, dst, send, recv, device):
+    return pltpu.make_async_remote_copy(
+        src_ref=src, dst_ref=dst, send_sem=send, recv_sem=recv,
+        device_id=device, device_id_type=MESH,
+    )
+
+
+class Leg:
+    def __init__(self, src, dst, device, send, recv):
+        self.ends = (src, dst, send, recv, device)
+
+    def start(self):
+        remote(*self.ends).start()
+
+    def wait_recv(self):
+        remote(*self.ends).wait_recv()
+
+    def wait_send(self):
+        remote(*self.ends).wait_send()
 
 
 class Copies:
     def __init__(self, send, recv):
         self.send, self.recv, self.used, self.open = send, recv, 0, []
 
-    def start(self, src, dst, device):
+    def make(self, src, dst, device):
         n = self.used
         self.used += 1
-        copy = pltpu.make_async_remote_copy(
-            src_ref=src,
-            dst_ref=dst,
-            send_sem=self.send.at[n],
-            recv_sem=self.recv.at[n],
-            device_id=device,
-            device_id_type=MESH,
-        )
+        copy = Leg(src, dst, device, self.send.at[n], self.recv.at[n])
+        self.open.append(copy)
+        return copy
+
+    def start(self, src, dst, device):
+        copy = self.make(src, dst, device)
         copy.start()
-        self.open.append(copy)
         return copy
 
     def retire(self, keep=0):
@@ -85,7 +103,7 @@
     meta, xin, meta_in, src, src_in, pad, res, WA, WU, WU2, WD, WD2, C, comp, around, H1, KV, Q,
     SB, RB, RC, mixed, H2, HID, SB2, RB2, RC2,
     result, swapped, sums, pooled, qkv_send, qkv_recv, new_send, new_all, last_send, last_recv,
-    local, big_send, big_recv, swap_send, swap_recv, s1, r1, s2, r2, s3, r3, s4, r4,
+    local, big_send, big_recv, swap_send, swap_recv, c_send, c_recv, side_send, side_recv, s1, r1, s2, r2, s3, r3, s4, r4,
 ):
     f = lax.axis_index("frame")
     t = lax.axis_index("tok")
@@ -121,6 +139,11 @@
     partner = dev(x, mod(z + 4, 8), y, 1 - c)
     after, before = (mod(f + 1, 32), t), (mod(f - 1, 32), t)
 
+    own_cache = x * 4 + zl
+
+    def all_of(ref, send, recv):
+        return remote(ref, ref, send, recv, sibling)
+
     barrier = pltpu.get_barrier_semaphore()
     friends = (xp, xm, yp, ym, zp, zm, sibling, partner, after, before)
     for friend in friends:
@@ -130,12 +153,6 @@
     copies = Copies(big_send, big_recv)
     moves = c != zh
 
-    def remote(src, dst, send, recv, device):
-        return pltpu.make_async_remote_copy(
-            src_ref=src, dst_ref=dst, send_sem=send, recv_sem=recv,
-            device_id=device, device_id_type=MESH,
-        )
-
     def swap(src, dst, n):
         return remote(src, dst, swap_send.at[n], swap_recv.at[n], partner)
 
@@ -148,11 +165,6 @@
     def _():
         swap(patches, xin, 0).start()
         swap(meta, meta_in, 1).start()
-
-    @pl.when(jnp.logical_not(moves))
-    def _():
-        xin[...] = patches[...]
-        meta_in[...] = meta[...]
 
     for load in loads[3:7]:
         load.wait()
@@ -279,7 +291,7 @@
             if tasks:
                 yield
 
-    load1, load4 = z_first(WA), x_first(C)
+    load1 = z_first(WA)
     load2 = both(z_first(WU), x_first(WU2))
     load3 = both(z_first(WD), x_first(WD2))
     ahead(load1, 1)
@@ -305,6 +317,8 @@
     for q in range(1, 4):
         mine = jnp.where(piece == float(q), quarters[q], mine)
     comp[...] = mine.astype(BF)
+    for q in range(4):
+        H1[0, :, q * QW : (q + 1) * QW] = quarters[q].astype(BF)
     hops = [
         copies.start(comp, around.at[0], after),
         copies.start(comp, around.at[1], before),
@@ -325,13 +339,52 @@
     )
     src[...] = source.astype(BF)
 
+    def gather(H):
+        a, b = pl.ds(0, 64), pl.ds(64, 64)
+        one = copies.make(H.at[0, a], H.at[3, a], yp)
+        two = copies.make(H.at[0, b], H.at[1, b], ym)
+        rest = [
+            copies.make(H.at[0, b], H.at[3, b], yp), copies.make(H.at[0, a], H.at[1, a], ym)
+        ]
+        far = [
+            copies.make(H.at[3, a], H.at[2, a], yp), copies.make(H.at[1, b], H.at[2, b], ym)
+        ]
+
+        def begin():
+            for copy in (one, two, *rest):
+                copy.start()
+
+        def forward():
+            one.wait_recv()
+            far[0].start()
+            two.wait_recv()
+            far[1].start()
+
+        def near():
+            for copy in rest:
+                copy.wait_recv()
+
+        def last():
+            for copy in far:
+                copy.wait_recv()
+
+        return begin, forward, near, last
+
+    begin1, forward1, near1, last1 = gather(H1)
+    stays = jnp.logical_not(moves)
+
     @pl.when(moves)
     def _():
         swap(src, src_in, 2).start()
 
-    @pl.when(jnp.logical_not(moves))
-    def _():
-        src_in[...] = src[...]
+    @pl.when(stays)
+    def _():
+        for q in range(4):
+            columns = slice(q * QW, (q + 1) * QW)
+            H1[0, :, columns] = jnp.where(
+                piece == float(q), src[...].astype(F32), H1[0, :, columns].astype(F32)
+            ).astype(BF)
+        begin1()
 
     ahead(load1, 1)
 
@@ -356,52 +409,35 @@
     cosine, sine = cos_a * cos_b - sin_a * sin_b, sin_a * cos_b + cos_a * sin_b
     sine = jnp.where(lax.rem(iota((62, 176), 1), HD) < HD // 2, -sine, sine)
     raw = ck_in[...].astype(F32)
-    C[0, place(0), 0] = jnp.zeros((CACHE_ROWS, CACHE_COLS), BF)
-    C[0, place(0), 0, 0:62, 0:176] = (raw * cosine + turned(raw) * sine).astype(BF)
-    C[0, place(0), 0, 0:62, 256:432] = cv_in[...]
+    cache_row = jnp.concatenate(
+        [raw * cosine + turned(raw) * sine, cv_in[...].astype(F32), jnp.zeros((62, 32), F32)], axis=1
+    )
+    C[0, own_cache] = jnp.zeros((CACHE_ROWS, CACHE_COLS), BF)
+    C[0, own_cache, 0:62, :] = cache_row.astype(BF)
     ahead(load1, 2)
+
+    pl.when(stays)(forward1)
 
     @pl.when(moves)
     def _():
         swap(patches, xin, 0).wait()
         swap(meta, meta_in, 1).wait()
         swap(src, src_in, 2).wait()
-
-    quarters = padded(xin)
-    piece = as_column(meta_in[1:2, :])
-    for q in range(4):
-        H1[0, :, q * QW : (q + 1) * QW] = jnp.where(
-            piece == float(q), src_in[...].astype(F32), quarters[q]
-        ).astype(BF)
-
-    def gather(H):
-        a, b = pl.ds(0, 64), pl.ds(64, 64)
-        one = copies.start(H.at[0, a], H.at[3, a], yp)
-        two = copies.start(H.at[0, b], H.at[1, b], ym)
-        rest = [
-            copies.start(H.at[0, b], H.at[3, b], yp), copies.start(H.at[0, a], H.at[1, a], ym)
-        ]
-        yield
-        one.wait_recv()
-        far = [copies.start(H.at[3, a], H.at[2, a], yp)]
-        two.wait_recv()
-        far.append(copies.start(H.at[1, b], H.at[2, b], ym))
-        yield
-        for copy in rest:
-            copy.wait_recv()
-        yield
-        for copy in far:
-            copy.wait_recv()
-
-    rows1 = gather(H1)
-    ahead(rows1, 1)
+        quarters = padded(xin)
+        piece = as_column(meta_in[1:2, :])
+        for q in range(4):
+            H1[0, :, q * QW : (q + 1) * QW] = jnp.where(
+                piece == float(q), src_in[...].astype(F32), quarters[q]
+            ).astype(BF)
+        begin1()
+
     ahead(load2, 2)
-    ahead(rows1, 1)
+    pl.when(moves)(forward1)
     ahead(load1, 1)
     ahead(load2, 1)
-    ahead(rows1, 1)
+    near1()
     ahead(load2, 1)
-    drain(rows1)
+    last1()
     ahead(load1, 1)
     drain(load1)
     ahead(load2, 1)
@@ -507,11 +543,9 @@
         if n == 0:
             ahead(load2, 1)
             ahead(load3, 1)
-            ahead(load4, 1)
         elif n == 1:
             ahead(load3, 1)
             ahead(load2, 1)
-            ahead(load4, 1)
         else:
             ahead(load3, 1)
             drain(load2)
@@ -519,10 +553,17 @@
     total = scatter(attend, SB, RB, RC, True, beside_attention)
     mixed[...] = (res[...].astype(F32) + total).astype(BF)
     H2[0] = norm_padded(mixed[...].astype(F32), valid).astype(BF)
-    rows2 = gather(H2)
-    ahead(rows2, 1)
+    begin2, forward2, near2, last2 = gather(H2)
+    begin2()
+
+    @pl.loop(1, 16)
+    def _(k):
+        to = lax.rem(own_cache + k, 16)
+        spot = C.at[0, own_cache]
+        device = dev(lax.div(to, 4), zh * 4 + lax.rem(to, 4), y, c)
+        remote(spot, spot, c_send, c_recv, device).start()
+
     ahead(load3, 1)
-    ahead(load4, 1)
 
     def up(block, at):
         rows = H2[block]
@@ -543,10 +584,9 @@
         first, second = up(0, at)
         HID[at, :, 0:512] = first
         HID[at, :, 512:768] = second
-    ahead(rows2, 1)
+    forward2()
     copies.retire(24)
-    ahead(load4, 1)
-    ahead(rows2, 1)
+    near2()
     ahead(load3, 1)
     drain(load3)
 
@@ -554,8 +594,7 @@
         return up_down(block)
 
     def far_rows(block):
-        ahead(load4, 1)
-        drain(rows2)
+        last2()
         return up_down(block)
 
     def own_rows(block):
@@ -563,11 +602,10 @@
         return down(own[0], 0) + down(own[1], 1)
 
     def beside_mlp(n):
-        if n == 0:
-            ahead(load4, 1)
-        else:
-            ahead(load4, 1)
+        if n == 2:
             copies.retire(8)
+            all_of(C.at[0, pl.ds(0, 15)], c_send, c_recv).wait_recv()
+            remote(C.at[0], C.at[1], side_send, side_recv, sibling).start()
 
     calls = [near_rows, near_rows, far_rows, own_rows]
     total = scatter(lambda block: calls.pop(0)(block), SB2, RB2, RC2, False, beside_mlp)
@@ -595,9 +633,6 @@
     def share(k):
         return remote(sums, pooled.at[slot], s1, r1, (home, lax.rem(t + k, 8)))
 
-    def all_of(ref, send, recv):
-        return remote(ref, ref, send, recv, sibling)
-
     @pl.when(moves)
     def _():
         share(0).start()
@@ -615,7 +650,7 @@
     def _():
         swap(result, swapped, 3).start()
 
-    drain(load4)
+    remote(C.at[0], C.at[1], side_send, side_recv, sibling).wait_recv()
     for load in loads[13:]:
         load.wait()
 
@@ -668,7 +703,7 @@
 
     new_send[...] = jnp.zeros_like(new_send)
     new_send[:, 0:176] = rot(whole[1])
-    new_send[:, 256:432] = whole[2].astype(BF).astype(F32)
+    new_send[:, 176:352] = whole[2].astype(BF).astype(F32)
 
 
     @pl.loop(1, 32)
@@ -684,8 +719,7 @@
     )
     queries = jnp.concatenate([wide_query, jnp.zeros((8, 80), F32)], axis=1).astype(BF)
     count = 32 * CACHE_ROWS
-    cached = [C[:, lax.rem(k - zl + 8 + 2, 8)] for k in range(4)]
-    old_keys = jnp.concatenate([part[..., 0:256].reshape(-1, 256) for part in cached], axis=0)
+    old_keys = C[:, :, :, 0:256].reshape(count, 256)
     s_old = dot_nt(queries, old_keys)
     s_old = jnp.where(lax.rem(iota((8, count), 1), CACHE_ROWS) < 62, s_old, -1e30)
 
@@ -701,10 +735,10 @@
     p_old = jnp.where(lax.rem(iota((8, count), 1), CACHE_ROWS) < 62, p_old, 0.0)
     p_new = jnp.where(iota((8, 32), 1) <= f, p_new, 0.0)
     mass = jnp.sum(p_old, axis=1, keepdims=True) + jnp.sum(p_new, axis=1, keepdims=True)
-    old_values = jnp.concatenate([part[..., 256:512].reshape(-1, 256) for part in cached], axis=0)
-    o = dot(p_old.astype(BF), old_values) + dot(p_new.astype(BF), known[:, 256:512].astype(BF))
+    old_values = C[:, :, :, 128:384].reshape(count, 256)
+    o = dot(p_old.astype(BF), old_values) + dot(p_new.astype(BF), known[:, 128:384].astype(BF))
     o = o / mass
-    temporal = jnp.where(lane < HD, o[0:1, 0:176], o[1:2, 0:176])
+    temporal = jnp.where(lane < HD, o[0:1, 48:224], o[1:2, 48:224])
     part = dot(jnp.broadcast_to(temporal, (8, 176)).astype(BF), to_w[...])
     for k in range(8):
         last_send[k, :, 0:176] = part[0:1, k * 176 : k * 176 + 176]
@@ -729,6 +763,8 @@
         kept.start()
 
     copies.retire()
+    all_of(C.at[0, pl.ds(0, 15)], c_send, c_recv).wait_send()
+    remote(C.at[0], C.at[1], side_send, side_recv, sibling).wait_send()
 
     @pl.when(moves)
     def _():
@@ -788,7 +824,7 @@
             pltpu.VMEM((2, 8, 4, W_ROWS, 256), BF),
             pltpu.VMEM((2, 4, 8, W_ROWS, 512), BF),
             pltpu.VMEM((2, 8, 4, W_ROWS, 256), BF),
-            pltpu.VMEM((2, 8, 4, CACHE_ROWS, CACHE_COLS), BF),
+            pltpu.VMEM((2, 16, CACHE_ROWS, CACHE_COLS), BF),
             pltpu.VMEM((TOK, QW), BF),
             pltpu.VMEM((2, TOK, QW), BF),
             pltpu.VMEM((4, TOK, DP), BF),
@@ -816,6 +852,7 @@
             dma((len(operands),)),
             dma((BIG,)), dma((BIG,)),
             dma((4,)), dma((4,)),
+            dma, dma, dma, dma,
             dma, dma, dma, dma, dma, dma, dma, dma,
         ],
         compiler_params=pltpu.CompilerParams(

time: 149 us -> 152 us (1.020)
  Pallas kernels: 146 us -> 149 us
    pallas_call x1, Pallas kernels: 146 us -> 149 us  [call(): pl.pallas_call(kernel, out_shape=(jax.ShapeDtypeStruct((TOK, D), BF), jax...]
where the time goes in v5:
time: 152 us
  Pallas kernels  149 us (98%)
  local copies, waits for them, and re-layouts  2.31 us (2%)
    pallas_call x1, Pallas kernels, call(): pl.pallas_call(kernel, out_shape=(jax.ShapeDtypeStruct((TOK, D), BF), jax...  149 us

profile of v5, /device:TPU:1, one launch (start us, length us, event | category | flops | bytes accessed | tf_op | source)
XLA Modules:
  0.0 151.8 jit_solution(11040731394851770356)
XLA Ops:
  0.6 148.8 %shard_map.185 = (bf16[128,1408]{1,0:T(8,128)(2,1)}, bf16[1,176]{1,0:T(2,128)(2,1)}) custom-call(bf16[128,1408]{1,0:T(8,128)(2,1)} %bitcast.8, s32[1,128]{1,0:T(1,128)} %bitcast.11, s32[1,128]{1,0:T(1,128)} %bitcast.12, bf16[44,176]{1,0:T(8,128)(2,1)} %wq_hbm.1, bf16[44,176]{1,0:T(8,128)(2,1)} %wk_hbm.1, bf16[44,176]{1,0:T(8,128)(2,1)} %wv_hbm.1, ...), custom_call_target="tpu_custom_call" | custom-call | flops 8000000000 | bytes 20000000 | tf_op jit(solution)/shard_map/pallas_call | solution.py:805
  149.5 0.0 copy-start
  149.5 1.7 %copy.22 = bf16[1,128,1408]{2,1,0:T(8,128)(2,1)} copy(bf16[1,128,1408]{2,1,0:T(8,128)(2,1)} %bitcast.7) | data formatting | bytes 720896
  151.2 0.0 copy-done
  151.2 0.6 copy.23
Async XLA Ops:
  149.5 1.8 %copy-start = (bf16[1,176]{1,0:T(2,128)(2,1)S(1)}, bf16[1,176]{1,0:T(2,128)(2,1)}, u32[]{:S(2)}) copy-start(bf16[1,176]{1,0:T(2,128)(2,1)} %get-tuple-element.9) | copy-start | bytes 1060

commit v6 on v5

--- a/solution.py
+++ b/solution.py
@@ -97,10 +97,12 @@
 
 def kernel(
     patches_hbm, offset_hbm, piece_hbm, wq_hbm, wk_hbm, wv_hbm, wo_hbm, wu_hbm, wd_hbm,
-    tq_hbm, tk_hbm, tv_hbm, to_hbm, ck_hbm, cv_hbm, pos_hbm, table_hbm, turn_hbm,
+    tq_hbm, tk_hbm, tv_hbm, to_hbm, ck_hbm, cv_hbm, pos_hbm, table_hbm,
+    pad_hbm, grow_hbm, spread_hbm, wide_kv_hbm, wide_q_hbm, narrow_hbm, valid_hbm, turn_hbm,
     out, frame_out,
-    patches, offset_in, piece_in, wq, wk, wv, wo, wu, wd, tq_w, tk_w, tv_w, to_w, ck_in, cv_in, pos_in, table, turn,
-    meta, xin, meta_in, src, src_in, pad, res, WA, WU, WU2, WD, WD2, C, comp, around, H1, KV, Q,
+    patches, offset_in, piece_in, wq, wk, wv, wo, wu, wd, tq_w, tk_w, tv_w, to_w, ck_in, cv_in, pos_in, table,
+    pad, grow_in, spread, wide_kv_in, wide_q_in, narrow_in, valid_in, turn,
+    meta, xin, meta_in, src, src_in, res, WA, WU, WU2, WD, WD2, C, comp, around, H1, KV, Q,
     SB, RB, RC, mixed, H2, HID, SB2, RB2, RC2,
     result, swapped, sums, pooled, qkv_send, qkv_recv, new_send, new_all, last_send, last_recv,
     local, big_send, big_recv, swap_send, swap_recv, c_send, c_recv, side_send, side_recv, s1, r1, s2, r2, s3, r3, s4, r4,
@@ -121,6 +123,8 @@
                 (patches_hbm, patches), (offset_hbm, offset_in), (piece_hbm, piece_in),
                 (wq_hbm, wq), (wk_hbm, wk), (wv_hbm, wv), (wo_hbm, wo), (wu_hbm, wu), (wd_hbm, wd),
                 (ck_hbm, ck_in), (cv_hbm, cv_in), (pos_hbm, pos_in), (table_hbm, table),
+                (grow_hbm, grow_in), (spread_hbm, spread), (pad_hbm, pad), (valid_hbm, valid_in),
+                (wide_kv_hbm, wide_kv_in), (wide_q_hbm, wide_q_in), (narrow_hbm, narrow_in),
                 (turn_hbm.at[f], turn), (tq_hbm, tq_w), (tk_hbm, tk_w), (tv_hbm, tv_w), (to_hbm, to_w),
             )
         )
@@ -166,15 +170,12 @@
         swap(patches, xin, 0).start()
         swap(meta, meta_in, 1).start()
 
-    for load in loads[3:7]:
+    for load in loads[3:7] + loads[13:15]:
         load.wait()
-    grow = jnp.where(iota((48, 44), 0) == iota((48, 44), 1), 1.0, 0.0).astype(BF)
+    grow = grow_in[...]
     total = None
     for n, w in enumerate((wq, wk, wv, wo)):
-        to = jnp.where(
-            iota((176, WC), 0) + n * 176 == iota((176, WC), 1), 1.0, 0.0
-        ).astype(BF)
-        term = dot(dot(grow, w[...]).astype(BF), to)
+        term = dot(dot(grow, w[...]).astype(BF), spread[n])
         total = term if total is None else total + term
     WA[0, 0, place(0)] = total.astype(BF)
 
@@ -296,12 +297,9 @@
     load3 = both(z_first(WD), x_first(WD2))
     ahead(load1, 1)
 
-    for q, (start, size) in enumerate(WINDOWS):
-        r, k = iota((size, QW), 0) + start, iota((size, QW), 1)
-        at = lax.rem(k, 48)
-        hit = (r == 352 * q + lax.div(k, 48) * 44 + at) & (at < 44)
-        pad[q, 0:size, :] = jnp.where(hit, 1.0, 0.0).astype(BF)
-    valid = lax.rem(iota((1, DP), 1), 48) < 44
+    for load in loads[15:17]:
+        load.wait()
+    valid = valid_in[...] > 0.5
 
     def padded(rows):
         for q, (start, size) in enumerate(WINDOWS):
@@ -407,7 +405,6 @@
 
     (cos_a, sin_a), (cos_b, sin_b) = chosen(high, 0), chosen(spot - 64.0 * high, 1)
     cosine, sine = cos_a * cos_b - sin_a * sin_b, sin_a * cos_b + cos_a * sin_b
-    sine = jnp.where(lax.rem(iota((62, 176), 1), HD) < HD // 2, -sine, sine)
     raw = ck_in[...].astype(F32)
     cache_row = jnp.concatenate(
         [raw * cosine + turned(raw) * sine, cv_in[...].astype(F32), jnp.zeros((62, 32), F32)], axis=1
@@ -454,17 +451,9 @@
             pieces.append(B[(*spot, slice(None), slice(start, start + size))])
         return jnp.concatenate(pieces, axis=0)
 
-    def wider(rows, first, columns, start):
-        r, k = iota((rows, columns), 0) + first, iota((rows, columns), 1) + start
-        at = lax.rem(k, 128)
-        return jnp.where((r == lax.div(k, 128) * HD + at) & (at < HD), 1.0, 0.0).astype(BF)
-
-    wide_q, wide_kv = wider(256, 0, 256, 0), wider(512, 128, 512, 256)
-    r, k = iota((256, 256), 1) + 512, iota((256, 256), 0)
-    at = lax.rem(k, 128)
-    narrow = jnp.where(
-        (r == 528 + lax.div(k, 128) * HD + at) & (at < HD), 1.0, 0.0
-    ).astype(BF)
+    for load in loads[17:20]:
+        load.wait()
+    wide_kv, wide_q, narrow = wide_kv_in[...], wide_q_in[...], narrow_in[...]
 
     rows = H1[...].reshape(4 * TOK, DP)
     sides = []
@@ -651,7 +640,7 @@
         swap(result, swapped, 3).start()
 
     remote(C.at[0], C.at[1], side_send, side_recv, sibling).wait_recv()
-    for load in loads[13:]:
+    for load in loads[20:]:
         load.wait()
 
     @pl.when(moves)
@@ -721,7 +710,7 @@
     count = 32 * CACHE_ROWS
     old_keys = C[:, :, :, 0:256].reshape(count, 256)
     s_old = dot_nt(queries, old_keys)
-    s_old = jnp.where(lax.rem(iota((8, count), 1), CACHE_ROWS) < 62, s_old, -1e30)
+    s_old = jnp.where((iota((8, count), 1) & (CACHE_ROWS - 1)) < 62, s_old, -1e30)
 
     all_of(new_all.at[pl.ds(0, 31)], s3, r3).wait_recv()
     known = new_all[:, 0, :]
@@ -732,7 +721,7 @@
     )
     p_old = jnp.exp2(s_old * RATE - top * RATE)
     p_new = jnp.exp2(s_new * RATE - top * RATE)
-    p_old = jnp.where(lax.rem(iota((8, count), 1), CACHE_ROWS) < 62, p_old, 0.0)
+    p_old = jnp.where((iota((8, count), 1) & (CACHE_ROWS - 1)) < 62, p_old, 0.0)
     p_new = jnp.where(iota((8, 32), 1) <= f, p_new, 0.0)
     mass = jnp.sum(p_old, axis=1, keepdims=True) + jnp.sum(p_new, axis=1, keepdims=True)
     old_values = C[:, :, :, 128:384].reshape(count, 256)
@@ -817,7 +806,6 @@
             pltpu.VMEM((2, TOK), F32),
             pltpu.VMEM((TOK, QW), BF),
             pltpu.VMEM((TOK, QW), BF),
-            pltpu.VMEM((4, 512, QW), BF),
             pltpu.VMEM((TOK, DP), BF),
             pltpu.VMEM((2, 4, 8, W_ROWS, WC), BF),
             pltpu.VMEM((2, 4, 8, W_ROWS, 512), BF),
@@ -864,6 +852,34 @@
     )(*operands)
 
 
+def constants():
+    grow = np.arange(48)[:, None] == np.arange(44)[None, :]
+    spread = np.stack(
+        [np.arange(176)[:, None] + n * 176 == np.arange(WC)[None, :] for n in range(4)]
+    )
+    pad = np.zeros((4, 512, QW), bool)
+    k = np.arange(QW)
+    for q, (start, size) in enumerate(WINDOWS):
+        at = k % 48
+        row = 352 * q + k // 48 * 44 + at - start
+        pad[q, :size] = (np.arange(size)[:, None] == row[None, :]) & (at < 44)[None, :]
+
+    def wider(rows, first, columns, start):
+        k = np.arange(columns) + start
+        at = k % 128
+        row = k // 128 * HD + at - first
+        return (np.arange(rows)[:, None] == row[None, :]) & (at < HD)[None, :]
+
+    valid = (np.arange(DP) % 48 < 44)[None, :]
+    narrow = wider(256, -16, 256, 0).T
+    held = [jnp.asarray(a.astype(np.float32), BF) for a in (pad, grow, spread)]
+    heads = [
+        jnp.asarray(a.astype(np.float32), BF)
+        for a in (wider(512, 128, 512, 256), wider(256, 0, 256, 0), narrow)
+    ]
+    return (*held, *heads, jnp.asarray(valid.astype(np.float32)))
+
+
 def body(
     patches, shift_offset, shift_slice, w_query, w_key, w_value, w_out, w_up, w_down,
     t_query, t_key, t_value, t_out, cache_keys, cache_values, cache_pos,
@@ -880,16 +896,17 @@
         axis=1,
     ).astype(np.float32)
     steps = np.arange(64)[:, None] * (10000.0 ** (-np.arange(half) / half))[None, :]
+    sign = np.where(np.arange(2 * HD) % HD < half, -1.0, 1.0)
     table = np.stack(
         [
-            np.concatenate([np.cos(64 * steps)] * 4 + [np.sin(64 * steps)] * 4, axis=1),
-            np.concatenate([np.cos(steps)] * 4 + [np.sin(steps)] * 4, axis=1),
+            np.concatenate([np.tile(np.cos(a), 4), np.tile(np.sin(a), 4) * sign], axis=1)
+            for a in (64 * steps, steps)
         ]
     ).astype(np.float32)
     patch_out, frame_out = call(
         patches[0], shift_offset[None], shift_slice[None], w_query, w_key, w_value,
         w_out.T, w_up, w_down.T, t_query, t_key, t_value, t_out, cache_keys, cache_values, cache_pos[None],
-        jnp.asarray(table), jnp.asarray(turn),
+        jnp.asarray(table), *constants(), jnp.asarray(turn),
     )
     return (patch_out[None], frame_out)
 

time: 152 us -> 154 us (1.013)
  no operation moved by 1% of the time
where the time goes in v6:
time: 154 us
  Pallas kernels  150 us (97%)
  local copies, waits for them, and re-layouts  2.95 us (2%)
    pallas_call x1, Pallas kernels, call(): pl.pallas_call(kernel, out_shape=(jax.ShapeDtypeStruct((TOK, D), BF), jax...  150 us

profile of v6, /device:TPU:1, one launch (start us, length us, event | category | flops | bytes accessed | tf_op | source)
XLA Modules:
  0.0 153.5 jit_solution(10966510584017467520)
XLA Ops:
  0.6 149.9 %shard_map.248 = (bf16[128,1408]{1,0:T(8,128)(2,1)}, bf16[1,176]{1,0:T(2,128)(2,1)}) custom-call(bf16[128,1408]{1,0:T(8,128)(2,1)} %bitcast.8, s32[1,128]{1,0:T(1,128)} %bitcast.11, s32[1,128]{1,0:T(1,128)} %bitcast.12, bf16[44,176]{1,0:T(8,128)(2,1)} %wq_hbm.1, bf16[44,176]{1,0:T(8,128)(2,1)} %wk_hbm.1, bf16[44,176]{1,0:T(8,128)(2,1)} %wv_hbm.1, ...), custom_call_target="tpu_custom_call" | custom-call | flops 8000000000 | bytes 20000000 | tf_op jit(solution)/shard_map/pallas_call | solution.py:794
  150.6 1.7 %copy.29 = bf16[1,128,1408]{2,1,0:T(8,128)(2,1)} copy(bf16[1,128,1408]{2,1,0:T(8,128)(2,1)} %bitcast.7) | data formatting | bytes 720896
  152.3 1.2 copy.30

commit v7 on v5

--- a/solution.py
+++ b/solution.py
@@ -100,7 +100,7 @@
     tq_hbm, tk_hbm, tv_hbm, to_hbm, ck_hbm, cv_hbm, pos_hbm, table_hbm, turn_hbm,
     out, frame_out,
     patches, offset_in, piece_in, wq, wk, wv, wo, wu, wd, tq_w, tk_w, tv_w, to_w, ck_in, cv_in, pos_in, table, turn,
-    meta, xin, meta_in, src, src_in, pad, res, WA, WU, WU2, WD, WD2, C, comp, around, H1, KV, Q,
+    meta, xin, meta_in, src, src_in, pad, res, WA, WU, WD, C, comp, around, H1, KV, Q,
     SB, RB, RC, mixed, H2, HID, SB2, RB2, RC2,
     result, swapped, sums, pooled, qkv_send, qkv_recv, new_send, new_all, last_send, last_recv,
     local, big_send, big_recv, swap_send, swap_recv, c_send, c_recv, side_send, side_recv, s1, r1, s2, r2, s3, r3, s4, r4,
@@ -292,8 +292,7 @@
                 yield
 
     load1 = z_first(WA)
-    load2 = both(z_first(WU), x_first(WU2))
-    load3 = both(z_first(WD), x_first(WD2))
+    load2, load3 = z_first(WU), z_first(WD)
     ahead(load1, 1)
 
     for q, (start, size) in enumerate(WINDOWS):
@@ -325,10 +324,8 @@
     ]
     for load in loads[7:9]:
         load.wait()
-    for w, one, two in ((wu, WU, WU2), (wd, WD, WD2)):
-        rows = dot(grow, w[...]).astype(BF)
-        one[0, 0, place(0)] = rows[:, 0:512]
-        two[0, place(0), 0] = rows[:, 512:768]
+    for w, one in ((wu, WU), (wd, WD)):
+        one[0, 0, place(0)] = dot(grow, w[...]).astype(BF)
     ahead(load1, 1)
     for copy in hops:
         copy.wait_recv()
@@ -566,24 +563,16 @@
     ahead(load3, 1)
 
     def up(block, at):
-        rows = H2[block]
-        return [
-            jax.nn.gelu(dot(rows, weight(WU, at, 0, 512))).astype(BF),
-            jax.nn.gelu(dot(rows, weight(WU2, at, 0, 256))).astype(BF),
-        ]
+        return jax.nn.gelu(dot(H2[block], weight(WU, at, 0, 768))).astype(BF)
 
     def down(hidden, at):
-        return dot_nt(hidden[0], weight(WD, at, 0, 512)) + dot_nt(
-            hidden[1], weight(WD2, at, 0, 256)
-        )
+        return dot_nt(hidden, weight(WD, at, 0, 768))
 
     def up_down(block):
         return down(up(block, 0), 0) + down(up(block, 1), 1)
 
     for at in range(2):
-        first, second = up(0, at)
-        HID[at, :, 0:512] = first
-        HID[at, :, 512:768] = second
+        HID[at] = up(0, at)
     forward2()
     copies.retire(24)
     near2()
@@ -598,8 +587,7 @@
         return up_down(block)
 
     def own_rows(block):
-        own = [(HID[at, :, 0:512], HID[at, :, 512:768]) for at in range(2)]
-        return down(own[0], 0) + down(own[1], 1)
+        return down(HID[0], 0) + down(HID[1], 1)
 
     def beside_mlp(n):
         if n == 2:
@@ -820,10 +808,8 @@
             pltpu.VMEM((4, 512, QW), BF),
             pltpu.VMEM((TOK, DP), BF),
             pltpu.VMEM((2, 4, 8, W_ROWS, WC), BF),
-            pltpu.VMEM((2, 4, 8, W_ROWS, 512), BF),
-            pltpu.VMEM((2, 8, 4, W_ROWS, 256), BF),
-            pltpu.VMEM((2, 4, 8, W_ROWS, 512), BF),
-            pltpu.VMEM((2, 8, 4, W_ROWS, 256), BF),
+            pltpu.VMEM((2, 4, 8, W_ROWS, WC), BF),
+            pltpu.VMEM((2, 4, 8, W_ROWS, WC), BF),
             pltpu.VMEM((2, 16, CACHE_ROWS, CACHE_COLS), BF),
             pltpu.VMEM((TOK, QW), BF),
             pltpu.VMEM((2, TOK, QW), BF),

time: 152 us -> 155 us (1.020)
  Pallas kernels: 149 us -> 152 us
    pallas_call x1, Pallas kernels: 149 us -> 152 us  [call(): pl.pallas_call(kernel, out_shape=(jax.ShapeDtypeStruct((TOK, D), BF), jax...]
where the time goes in v7:
time: 155 us
  Pallas kernels  152 us (98%)
  local copies, waits for them, and re-layouts  2.31 us (1%)
    pallas_call x1, Pallas kernels, call(): pl.pallas_call(kernel, out_shape=(jax.ShapeDtypeStruct((TOK, D), BF), jax...  152 us

profile of v7, /device:TPU:1, one launch (start us, length us, event | category | flops | bytes accessed | tf_op | source)
XLA Modules:
  0.0 154.7 jit_solution(15219597391921721956)
XLA Ops:
  0.6 151.7 %shard_map.185 = (bf16[128,1408]{1,0:T(8,128)(2,1)}, bf16[1,176]{1,0:T(2,128)(2,1)}) custom-call(bf16[128,1408]{1,0:T(8,128)(2,1)} %bitcast.8, s32[1,128]{1,0:T(1,128)} %bitcast.11, s32[1,128]{1,0:T(1,128)} %bitcast.12, bf16[44,176]{1,0:T(8,128)(2,1)} %wq_hbm.1, bf16[44,176]{1,0:T(8,128)(2,1)} %wk_hbm.1, bf16[44,176]{1,0:T(8,128)(2,1)} %wv_hbm.1, ...), custom_call_target="tpu_custom_call" | custom-call | flops 8000000000 | bytes 20000000 | tf_op jit(solution)/shard_map/pallas_call | solution.py:793
  152.4 0.0 copy-start
  152.4 1.7 %copy.22 = bf16[1,128,1408]{2,1,0:T(8,128)(2,1)} copy(bf16[1,128,1408]{2,1,0:T(8,128)(2,1)} %bitcast.7) | data formatting | bytes 720896
  154.1 0.0 copy-done
  154.1 0.6 copy.23
Async XLA Ops:
  152.4 1.8 %copy-start = (bf16[1,176]{1,0:T(2,128)(2,1)S(1)}, bf16[1,176]{1,0:T(2,128)(2,1)}, u32[]{:S(2)}) copy-start(bf16[1,176]{1,0:T(2,128)(2,1)} %get-tuple-element.9) | copy-start | bytes 1060
